TPU v7x, 768 devices: a whole 4x8x12 slice. The times are simulated.
768 devices in a mesh: row: 96 (over x, y, z_lo), feat: 8 (over z_hi, core).
Axes of the slice: x: 4, y: 8, z: 12 (z_hi: 4, z_lo: 3; z = z_hi * 3 + z_lo), core: 2. Of those that a mesh axis runs over, the one named last changes fastest.
Arguments:
- features: bfloat16 [24576, 128], P('row', 'feat'), may hold values from -6 to 6
- weight: bfloat16 [128, 256], P('feat'), may hold values from -0.5 to 0.5
- norm_scale: float32 [24576], P('row'), may hold values from 0.3 to 3
- tile_rows: int32 [4608], P('row'), may hold values from 0 to 1
- tile_cols: int32 [4608], P('row'), may hold values from 0 to 191
- tile_vals: bfloat16 [4608, 128, 128], P('row'), may hold values from -0.109375 to 0.109375
- cotangent: bfloat16 [24576, 256], P('row', 'feat'), may hold values from -6 to 6
Outputs:
- activated: bfloat16 [24576, 256], P('row', 'feat')
- weight_grad: float32 [128, 256], P('feat')
- feature_grad: bfloat16 [24576, 128], P('row', 'feat')
Inputs may be any that keep to these rules, and one draw needn't show every extreme that they name: `tile_cols`: tiles may repeat a coordinate; repeated tiles add.
All inputs are finite; a program needn't handle non-finite values.
Results may differ from a plain program's by a relative error of at most 0.0068.
Values may be sent and summed in bfloat16 or wider, within the bound.
No kernel may reach another device: no remote copies, remote signals or barrier semaphores. Data moves between devices by JAX's collectives and lax.ppermute only.
A program may use at most 64 MiB of HBM per device.

v0:
```python
import jax
import jax.numpy as jnp
from jax import lax
from jax.sharding import PartitionSpec as P


def per_device(features, weight, norm_scale, tile_rows, tile_cols, tile_vals, cotangent):
    rows_dev = features.shape[0]
    tile_len = tile_vals.shape[1]
    row_tiles = rows_dev // tile_len
    hid_part = cotangent.shape[1]
    highest = lax.Precision.HIGHEST
    scaled = norm_scale[:, None]
    partial_value = jnp.dot(features, weight, preferred_element_type=jnp.float32)
    shared = lax.psum_scatter(partial_value, "feat", scatter_dimension=1, tiled=True)
    source = (shared * scaled).astype(jnp.bfloat16)
    within = jnp.arange(tile_len, dtype=jnp.int32)
    global_rows = tile_cols[:, None] * tile_len + within[None, :]
    row_select = (tile_rows[None, :] == jnp.arange(row_tiles, dtype=jnp.int32)[:, None]).astype(
        jnp.float32
    )
    empty = jnp.zeros((tile_cols.shape[0], tile_len, hid_part), jnp.bfloat16)
    rows_piece = lax.all_gather(source, "row", axis=0, tiled=True)
    piece_len = rows_piece.shape[0]
    offset = global_rows
    inside = (offset >= 0) & (offset < piece_len)
    fetched = rows_piece[jnp.clip(offset, 0, piece_len - 1)]
    picked_rows = jnp.where(inside[:, :, None], fetched, empty)
    contrib = jnp.einsum("tij,tjh->tih", tile_vals, picked_rows, preferred_element_type=jnp.float32)
    summed = jnp.einsum("rt,tih->rih", row_select, contrib, precision=highest)
    pre_act = summed.reshape(rows_dev, hid_part) * scaled
    activated = jax.nn.silu(pre_act).astype(jnp.bfloat16)
    sigma = jax.nn.sigmoid(pre_act)
    slope = sigma * (1.0 + pre_act * (1.0 - sigma))
    back_in = (cotangent.astype(jnp.float32) * slope * scaled).astype(jnp.bfloat16)
    back_tiles = back_in.reshape(row_tiles, tile_len, hid_part)[tile_rows]
    back_terms = jnp.einsum(
        "tji,tjh->tih", tile_vals, back_tiles, preferred_element_type=jnp.float32
    ).reshape(-1, hid_part)
    flat_rows = global_rows.reshape(-1)
    offset = flat_rows
    inside = (offset >= 0) & (offset < rows_dev * lax.axis_size("row"))
    kept = jnp.where(inside[:, None], back_terms, jnp.zeros((), jnp.float32))
    grad_source = lax.psum_scatter(
        jax.ops.segment_sum(
            kept,
            jnp.clip(offset, 0, rows_dev * lax.axis_size("row") - 1),
            num_segments=rows_dev * lax.axis_size("row"),
        ),
        "row",
        scatter_dimension=0,
        tiled=True,
    )
    grad_proj = (grad_source * scaled).astype(jnp.bfloat16)
    grad_full = lax.all_gather(grad_proj, "feat", axis=1, tiled=True)
    weight_part = lax.dot_general(
        features, grad_full, (((0,), (0,)), ((), ())), preferred_element_type=jnp.float32
    )
    weight_grad = lax.psum(weight_part, "row")
    feature_grad = lax.dot_general(
        grad_full, weight, (((1,), (1,)), ((), ())), preferred_element_type=jnp.float32
    ).astype(jnp.bfloat16)
    return (activated, weight_grad, feature_grad)


def solution(mesh):
    placed = (
        P("row", "feat"),
        P("feat", None),
        P("row"),
        P("row"),
        P("row"),
        P("row", None, None),
        P("row", "feat"),
    )
    return jax.shard_map(
        per_device,
        mesh=mesh,
        in_specs=placed,
        out_specs=(P("row", "feat"), P("feat", None), P("row", "feat")),
        check_vma=False,
    )
```

profile of v0, /device:TPU:192, one launch (start us, length us, event | category | flops | bytes accessed | tf_op | source)
XLA Modules:
  0.0 1718.7 jit_solution(11890523037329619199)
XLA Ops:
  7.2 0.0 copy-start
  7.2 0.0 reduce-scatter.3.cloned.1.call-start
  7.2 1.7 fusion.19
  9.0 0.0 reduce-scatter.3.cloned.1.call-update
  9.0 0.0 all-gather.2.cloned.1.call-start
  9.0 49.1 %reduce-scatter.3.cloned.1.call-done = f32[256,32]{0,1:T(8,128)} async-done(((f32[256,256]{0,1:T(8,128)}), f32[256,32]{0,1:T(8,128)}) %reduce-scatter.3.cloned.1.call-update) | async-done | bytes 32784 | tf_op jit(solution)/shard_map/reduce_scatter | solution.py:15
  58.1 1.4 multiply_convert_fusion.3
  59.5 0.0 all-gather.2.cloned.1.call-update
  59.5 0.0 reduce-scatter.5.cloned.1.call-start
  59.6 0.7 compare_select_fusion.1
  60.2 0.6 pad_clamp_fusion
  60.8 0.7 broadcast_multiply_fusion
  61.5 0.1 fusion.18
  61.6 0.7 clamp_bitcast_fusion
  62.3 0.1 fusion.8
  62.3 416.1 %all-gather.2.cloned.1.call-done = bf16[24576,32]{0,1:T(8,128)(2,1)} async-done(((bf16[256,32]{0,1:T(8,128)(2,1)}), bf16[24576,32]{0,1:T(8,128)(2,1)}) %all-gather.2.cloned.1.call-update) | async-done | bytes 1572880 | tf_op jit(solution)/shard_map/all_gather | solution.py:23
  478.5 6.3 copy.15
  484.7 20.0 %gather_fusion = bf16[6144,32]{1,0:T(8,128)(2,1)S(1)} fusion(bf16[24576,32]{1,0:T(8,128)(2,1)} %copy.15, s32[6144]{0:T(1024)S(1)} %fusion.8), kind=kCustom, calls=%fused_computation | custom fusion | bytes 811008 | tf_op jit(solution)/shard_map/gather | solution.py:27
  504.8 0.7 copy.16
  505.5 0.0 copy-start.3
  505.5 0.0 copy-done
  505.5 0.9 convolution_bitcast_fusion.1
  506.4 1.5 fusion.2
  507.9 0.0 copy-done.3
  507.9 1.3 fusion.12
  509.2 0.7 gather_fusion.1
  510.0 0.5 convolution_bitcast_fusion
  510.5 0.1 bitcast_select_fusion
  510.6 2.2 copy.20
  512.8 38.8 %scatter_custom_fusion = f32[24576,32]{1,0:T(8,128)} fusion(s32[6144]{0:T(1024)} %clamp_bitcast_fusion, f32[6144,32]{1,0:T(8,128)} %copy.20, f32[]{:T(128)} %constant.1.clone.1), kind=kCustom, calls=%fused_computation.3 | custom fusion | flops 196608 | bytes 3146240 | tf_op jit(solution)/shard_map/scatter-add | solution.py:45
  551.5 8.8 copy.21
  560.4 0.0 copy-start.4
  560.4 0.0 copy-start.1
  560.4 0.0 copy-start.2
  560.4 0.0 reduce-scatter.5.cloned.1.call-update
  560.4 576.3 %reduce-scatter.5.cloned.1.call-done = f32[256,32]{0,1:T(8,128)} async-done(((f32[24576,32]{0,1:T(8,128)}), f32[256,32]{0,1:T(8,128)}) %reduce-scatter.5.cloned.1.call-update) | async-done | bytes 32784 | tf_op jit(solution)/shard_map/reduce_scatter | solution.py:44
  1136.7 0.0 copy-done.4
  1136.7 0.8 multiply_convert_fusion
  1137.4 16.3 all_gather.7
  1153.8 0.0 copy-done.1
  1153.8 0.7 convolution_convert_fusion
  1154.5 0.0 copy-done.2
  1154.5 0.1 convolution_bitcast_fusion.2
  1154.7 557.5 %psum.7 = f32[16,256]{1,0:T(8,128)} all-reduce(f32[16,256]{1,0:T(8,128)S(1)} %convolution_bitcast_fusion.2), channel_id=1, replica_groups=mesh['row'=96,'feat'=8] {'row'}, use_global_device_ids=true, to_apply=%region_3.4 | all-reduce | flops 4096 | bytes 32768 | tf_op jit(solution)/shard_map/psum | solution.py:59
  (1 shorter events, 0.0 us)
Async XLA Ops:
  7.2 498.3 %copy-start = (bf16[48,128,128]{2,1,0:T(8,128)(2,1)S(1)}, bf16[48,128,128]{2,1,0:T(8,128)(2,1)}, u32[]{:S(2)}) copy-start(bf16[48,128,128]{2,1,0:T(8,128)(2,1)} %param.12) | copy-start | bytes 4718596
  7.2 51.0 %reduce-scatter.3.cloned.1.call-start = ((), (), s32[]{:S(2)}) async-start(), calls=%async_computation.2 | async-start | bytes 294912 | tf_op jit(solution)/shard_map/reduce_scatter | solution.py:15
  9.0 469.5 %all-gather.2.cloned.1.call-start = ((), (), s32[]{:S(2)}) async-start(), calls=%async_computation.3 | async-start | bytes 1589248 | tf_op jit(solution)/shard_map/all_gather | solution.py:23
  59.5 1077.1 %reduce-scatter.5.cloned.1.call-start = ((), (), s32[]{:S(2)}) async-start(), calls=%async_computation.4 | async-start | bytes 3178496 | tf_op jit(solution)/shard_map/reduce_scatter | solution.py:44
  505.5 2.4 copy-start.3
  560.4 576.3 %copy-start.4 = (f32[256]{0:T(256)S(1)}, f32[256]{0:T(256)}, u32[]{:S(2)}) copy-start(f32[256]{0:T(256)} %param.9) | copy-start | bytes 3076
  560.4 593.4 %copy-start.1 = (bf16[16,256]{1,0:T(8,128)(2,1)S(1)}, bf16[16,256]{1,0:T(8,128)(2,1)}, u32[]{:S(2)}) copy-start(bf16[16,256]{1,0:T(8,128)(2,1)} %param.8) | copy-start | bytes 24580
  560.4 594.1 %copy-start.2 = (bf16[256,16]{0,1:T(8,128)(2,1)S(1)}, bf16[256,16]{0,1:T(8,128)(2,1)}, u32[]{:S(2)}) copy-start(bf16[256,16]{0,1:T(8,128)(2,1)} %param.7) | copy-start | bytes 24580
Sparse Core Ops, SparseCore 0:
  11.1 47.0 reduce-scatter.2
  61.3 417.1 all-gather.1
  560.5 576.1 reduce-scatter.4
where the time goes:
time: 1720 us
  waiting for transfers between devices  1040 us (60%)
  blocking collectives  574 us (33%)
  other arithmetic  45 us (3%)
  local copies, waits for them, and re-layouts  38.8 us (2%)
    reduce_scatter x1, waiting for transfers between devices, per_device(): lax.psum_scatter(jax.ops.segment_sum(kept, jnp.clip(offset, 0, rows_dev *...  576 us
    psum x1, blocking collectives, per_device(): weight_grad = lax.psum(weight_part, 'row')  558 us
    all_gather x1, waiting for transfers between devices, per_device(): rows_piece = lax.all_gather(source, 'row', axis=0, tiled=True)  416 us
    reduce_scatter x1, waiting for transfers between devices, per_device(): lax.psum_scatter(partial_value, 'feat', scatter_dimension=1, tiled=True)  49.1 us
    scatter-add x1, other arithmetic, per_device(): jax.ops.segment_sum(kept, jnp.clip(offset, 0, rows_dev * lax.axis_size('r...  38.8 us
  transfers between devices with their start and end apart: 3, of which 3 were waited for; matrix products, arithmetic and copies ran while one was open for 0% of the time, Pallas kernels for 0%

commit v1 on v0

v1 whole, which is shorter than its diff:
```python
import jax
import jax.numpy as jnp
from jax import lax
from jax.experimental import pallas as pl
from jax.experimental.pallas import tpu as pltpu
from jax.sharding import PartitionSpec as P

F32 = jnp.float32
BF16 = jnp.bfloat16
NT = (((1,), (1,)), ((), ()))
NN = (((1,), (0,)), ((), ()))


def halves(value):
    head = value.astype(BF16)
    return head, (value - head.astype(F32)).astype(BF16)


def forward_kernel(rows_ref, cols_ref, tiles_ref, nodes_ref, sum_ref):
    row_tiles = sum_ref.shape[0]
    totals = [jnp.zeros(sum_ref.shape[1:], F32) for _ in range(row_tiles)]
    for t in range(tiles_ref.shape[0]):
        term = lax.dot_general(
            nodes_ref[cols_ref[t]], tiles_ref[t], NT, preferred_element_type=F32
        )
        for i in range(row_tiles):
            totals[i] = totals[i] + jnp.where(rows_ref[t] == i, term, 0.0)
    for i in range(row_tiles):
        sum_ref[i] = totals[i]


def backward_kernel(rows_ref, cols_ref, tiles_ref, back_ref, out_ref, total_ref):
    total_ref[...] = jnp.zeros_like(total_ref)
    for t in range(tiles_ref.shape[0]):
        total_ref[cols_ref[t]] += lax.dot_general(
            back_ref[rows_ref[t]], tiles_ref[t], NN, preferred_element_type=F32
        )
    out_ref[...] = total_ref[...].astype(out_ref.dtype)


def per_device(features, weight, norm_scale, tile_rows, tile_cols, tile_vals, cotangent):
    rows_dev, feat_part = features.shape
    tile_len = tile_vals.shape[1]
    row_tiles = rows_dev // tile_len
    hid_part = cotangent.shape[1]
    n_row = lax.axis_size("row")
    n_feat = lax.axis_size("feat")
    hidden = hid_part * n_feat
    me = lax.axis_index("feat")
    smem = pl.BlockSpec(memory_space=pltpu.SMEM)
    vmem = pl.BlockSpec(memory_space=pltpu.VMEM)

    def by_tile(value):
        return value.reshape(-1, row_tiles, tile_len).transpose(1, 0, 2)

    def by_row(value):
        return value.transpose(1, 0, 2).reshape(-1, rows_dev)

    scaled = by_tile((features.T.astype(F32) * norm_scale[None, :]).astype(BF16))
    nodes = lax.all_to_all(
        jnp.broadcast_to(scaled[None], (n_row,) + scaled.shape), "row", 0, 0
    ).reshape(n_row * row_tiles, feat_part, tile_len)
    mixed = pl.pallas_call(
        forward_kernel,
        out_shape=jax.ShapeDtypeStruct((row_tiles, feat_part, tile_len), F32),
        in_specs=[smem, smem, vmem, vmem],
        out_specs=vmem,
        compiler_params=pltpu.CompilerParams(vmem_limit_bytes=16 * 2**20),
    )(tile_rows, tile_cols, tile_vals, nodes)
    mixed = by_row(mixed)

    head, rest = halves(mixed)
    block = jnp.concatenate([head, rest, weight, cotangent.T], axis=0)
    group = lax.all_to_all(
        jnp.broadcast_to(block[None], (n_feat,) + block.shape), "feat", 0, 0
    )
    cuts = [feat_part, 2 * feat_part, 3 * feat_part]
    all_head, all_rest, all_weight, all_cot = jnp.split(group, cuts, axis=1)
    all_head = all_head.reshape(-1, rows_dev)
    all_rest = all_rest.reshape(-1, rows_dev)
    all_weight = all_weight.reshape(-1, hidden)
    all_cot = all_cot.reshape(hidden, rows_dev)

    tn = (((0,), (0,)), ((), ()))
    pre_act = (
        lax.dot_general(all_weight, all_head, tn, preferred_element_type=F32)
        + lax.dot_general(all_weight, all_rest, tn, preferred_element_type=F32)
    ) * norm_scale[None, :]
    sigma = jax.nn.sigmoid(pre_act)
    slope = sigma * (1.0 + pre_act * (1.0 - sigma))
    back_in = (all_cot.astype(F32) * slope * norm_scale[None, :]).astype(BF16)
    own = lax.dynamic_slice_in_dim(pre_act, me * hid_part, hid_part, 0)
    activated = jax.nn.silu(own).astype(BF16).T

    back = lax.dot_general(weight, back_in, NN, preferred_element_type=F32)
    col_terms = pl.pallas_call(
        backward_kernel,
        out_shape=jax.ShapeDtypeStruct((n_row * row_tiles, feat_part, tile_len), BF16),
        in_specs=[smem, smem, vmem, vmem],
        out_specs=vmem,
        scratch_shapes=[pltpu.VMEM((n_row * row_tiles, feat_part, tile_len), F32)],
        compiler_params=pltpu.CompilerParams(vmem_limit_bytes=16 * 2**20),
    )(tile_rows, tile_cols, tile_vals, by_tile(back.astype(BF16)))

    weight_part = (
        lax.dot_general(head, back_in, NT, preferred_element_type=F32)
        + lax.dot_general(rest, back_in, NT, preferred_element_type=F32)
    ).astype(BF16)
    sent = jnp.concatenate(
        [
            col_terms.reshape(n_row, row_tiles * feat_part, tile_len),
            jnp.broadcast_to(
                weight_part.reshape(1, -1, tile_len),
                (n_row, feat_part * hidden // tile_len, tile_len),
            ),
        ],
        axis=1,
    )
    got = lax.all_to_all(sent, "row", 0, 0)
    total = jnp.sum(got.astype(F32), axis=0)
    grad = by_row(total[: row_tiles * feat_part].reshape(row_tiles, feat_part, tile_len))
    weight_grad = total[row_tiles * feat_part :].reshape(feat_part, hidden)
    feature_grad = (grad * norm_scale[None, :]).astype(BF16).T
    return (activated, weight_grad, feature_grad)


def solution(mesh):
    placed = (
        P("row", "feat"),
        P("feat", None),
        P("row"),
        P("row"),
        P("row"),
        P("row", None, None),
        P("row", "feat"),
    )
    return jax.shard_map(
        per_device,
        mesh=mesh,
        in_specs=placed,
        out_specs=(P("row", "feat"), P("feat", None), P("row", "feat")),
        check_vma=False,
    )
```

time: 1720 us -> 127 us (0.07)
  the two profiles are of different devices: /device:TPU:192 before, /device:TPU:1 now
where the time goes in v1:
time: 127 us
  blocking collectives  72 us (57%)
  waiting for transfers between devices  39.4 us (31%)
  starting transfers between devices  6.11 us (5%)
  other arithmetic  3.72 us (3%)
  Pallas kernels  2.65 us (2%)
    all_to_all x1, waiting for transfers between devices, per_device(): got = lax.all_to_all(sent, 'row', 0, 0)  39.4 us
    all_to_all x1, blocking collectives, per_device(): lax.all_to_all(jnp.broadcast_to(scaled[None], (n_row,) + scaled.shape), '...  38.4 us
    all_to_all x1, blocking collectives, per_device(): lax.all_to_all(jnp.broadcast_to(block[None], (n_feat,) + block.shape), 'f...  33.6 us
    all_to_all x1, starting transfers between devices, per_device(): got = lax.all_to_all(sent, 'row', 0, 0)  6.11 us
  transfers between devices with their start and end apart: 1, of which 1 were waited for; matrix products, arithmetic and copies ran while one was open for 0% of the time, Pallas kernels for 0%

profile of v1, /device:TPU:1, one launch (start us, length us, event | category | flops | bytes accessed | tf_op | source)
XLA Modules:
  0.0 126.7 jit_solution(885486358531229803)
XLA Ops:
  0.6 0.0 copy-start
  0.6 0.0 copy-start.2
  0.7 0.0 copy-start.1
  0.7 0.8 fusion.13
  1.5 0.1 broadcast_in_dim.8
  1.6 38.4 %all_to_all.15 = bf16[96,2,16,128]{3,2,1,0:T(8,128)(2,1)S(1)} all-to-all(bf16[96,2,16,128]{3,2,1,0:T(8,128)(2,1)S(1)} %broadcast_in_dim.8), channel_id=1, replica_groups=mesh['row'=96,'feat'=8] {'row'}, dimensions={0} | all-to-all | bytes 1572864 | tf_op jit(solution)/shard_map/all_to_all | solution.py:60
  40.0 0.0 copy-start.3
  40.0 0.0 copy-start.4
  40.0 0.0 copy-done
  40.0 0.0 copy-done.2
  40.0 0.0 copy-done.1
  40.0 1.5 %shard_map.94 = f32[2,16,128]{2,1,0:T(8,128)S(1)} custom-call(s32[48]{0:T(128)S(1)} %copy-done.1, s32[48]{0:T(128)S(1)} %copy-done.2, bf16[48,128,128]{2,1,0:T(8,128)(2,1)S(1)} %copy-done, bf16[192,16,128]{2,1,0:T(8,128)(2,1)S(1)} %bitcast.62), custom_call_target="tpu_custom_call" | custom-call | tf_op jit(solution)/shard_map/pallas_call | solution.py:63
  41.5 0.0 copy-start.5
  41.5 0.0 copy-done.3
  41.5 0.0 copy-done.4
  41.6 33.6 %all_to_all.16 = bf16[8,80,256]{2,1,0:T(8,128)(2,1)S(1)} all-to-all(bf16[8,80,256]{2,1,0:T(8,128)(2,1)S(1)} %broadcast_in_dim.9), channel_id=1, replica_groups=mesh['row'=96,'feat'=8] {'feat'}, dimensions={0} | all-to-all | bytes 655360 | tf_op jit(solution)/shard_map/all_to_all | solution.py:74
  75.2 0.2 convolution_bitcast_fusion
  75.4 0.0 copy-done.5
  75.4 0.3 fusion.5
  75.8 0.1 fusion.15
  75.9 0.2 fusion.3
  76.1 0.2 fusion.2
  76.3 1.2 shard_map.95
  77.5 0.1 broadcast_in_dim.11
  77.6 1.4 %pad_maximum_fusion = bf16[96,64,128]{2,1,0:T(8,128)(2,1)} fusion(bf16[96,32,128]{2,1,0:T(8,128)(2,1)S(1)} %broadcast_in_dim.11, bf16[96,32,128]{2,1,0:T(8,128)(2,1)S(1)} %bitcast.63), kind=kLoop, calls=%fused_computation.1 | loop fusion | flops 3145728 | bytes 3145728 | tf_op jit(solution)/shard_map/concatenate | solution.py:109
  79.0 6.1 %all-to-all-start.2 = ((bf16[96,64,128]{2,1,0:T(8,128)(2,1)}), bf16[96,64,128]{2,1,0:T(8,128)(2,1)S(1)}, u32[]{:S(2)}, u32[]{:S(2)}) async-start(bf16[96,64,128]{2,1,0:T(8,128)(2,1)} %pad_maximum_fusion), calls=%async_computation.2 | async-start | bytes 3145728 | tf_op jit(solution)/shard_map/all_to_all | solution.py:119
  85.1 0.6 fusion.12
  85.8 39.4 %all-to-all-done.2 = bf16[96,64,128]{2,1,0:T(8,128)(2,1)S(1)} async-done(((bf16[96,64,128]{2,1,0:T(8,128)(2,1)}), bf16[96,64,128]{2,1,0:T(8,128)(2,1)S(1)}, u32[]{:S(2)}, u32[]{:S(2)}) %all-to-all-start.2) | async-done | bytes 1572896 | tf_op jit(solution)/shard_map/all_to_all | solution.py:119
  125.2 0.3 convert_reduce_fusion
  125.5 0.6 fusion.14
  126.1 0.6 reshape.46
  (10 shorter events, 0.1 us)
Async XLA Ops:
  0.6 39.4 %copy-start = (bf16[48,128,128]{2,1,0:T(8,128)(2,1)S(1)}, bf16[48,128,128]{2,1,0:T(8,128)(2,1)}, u32[]{:S(2)}) copy-start(bf16[48,128,128]{2,1,0:T(8,128)(2,1)} %tiles_ref.3) | copy-start | bytes 4718596
  0.6 39.4 %copy-start.2 = (s32[48]{0:T(128)S(1)}, s32[48]{0:T(128)}, u32[]{:S(2)}) copy-start(s32[48]{0:T(128)} %cols_ref.3) | copy-start | bytes 580
  0.7 39.3 %copy-start.1 = (s32[48]{0:T(128)S(1)}, s32[48]{0:T(128)}, u32[]{:S(2)}) copy-start(s32[48]{0:T(128)} %rows_ref.3) | copy-start | bytes 580
  40.0 1.5 %copy-start.3 = (bf16[16,256]{1,0:T(8,128)(2,1)S(1)}, bf16[16,256]{1,0:T(8,128)(2,1)}, u32[]{:S(2)}) copy-start(bf16[16,256]{1,0:T(8,128)(2,1)} %param.8) | copy-start | bytes 24580
  40.0 1.5 %copy-start.4 = (bf16[256,32]{0,1:T(8,128)(2,1)S(1)}, bf16[256,32]{0,1:T(8,128)(2,1)}, u32[]{:S(2)}) copy-start(bf16[256,32]{0,1:T(8,128)(2,1)} %param.13) | copy-start | bytes 49156
  41.5 34.0 %copy-start.5 = (f32[256]{0:T(256)S(1)}, f32[256]{0:T(256)}, u32[]{:S(2)}) copy-start(f32[256]{0:T(256)} %param.9) | copy-start | bytes 3076
  79.0 46.2 %all-to-all-start.2 = ((bf16[96,64,128]{2,1,0:T(8,128)(2,1)}), bf16[96,64,128]{2,1,0:T(8,128)(2,1)S(1)}, u32[]{:S(2)}, u32[]{:S(2)}) async-start(bf16[96,64,128]{2,1,0:T(8,128)(2,1)} %pad_maximum_fusion), calls=%async_computation.2 | async-start | bytes 3145728 | tf_op jit(solution)/shard_map/all_to_all | solution.py:119

commit v2 on v0

v2 whole, which is shorter than its diff:
```python
import functools

import jax
import jax.numpy as jnp
from jax import lax
from jax.experimental import pallas as pl
from jax.experimental.pallas import tpu as pltpu
from jax.sharding import Mesh, PartitionSpec as P

F32 = jnp.float32
BF16 = jnp.bfloat16
NT = (((1,), (1,)), ((), ()))
NN = (((1,), (0,)), ((), ()))
TN = (((0,), (0,)), ((), ()))
LANES = 128


def halves(value):
    head = value.astype(BF16)
    return head, (value - head.astype(F32)).astype(BF16)


def dot(left, right, dims):
    return lax.dot_general(left, right, dims, preferred_element_type=F32)


def start_kernel(features_ref, norm_ref, out_ref):
    scaled = (features_ref[...].astype(F32) * norm_ref[...]).astype(BF16)
    for n in range(out_ref.shape[0]):
        for i in range(out_ref.shape[1]):
            out_ref[n, i] = scaled[:, i * LANES : (i + 1) * LANES]


def forward_kernel(rows_ref, cols_ref, tiles_ref, nodes_ref, weight_ref, cot_ref, out_ref):
    part = weight_ref.shape[0]
    row_tiles = cot_ref.shape[1] // LANES
    totals = [jnp.zeros((part, LANES), F32) for _ in range(row_tiles)]
    for t in range(tiles_ref.shape[0]):
        term = dot(nodes_ref[cols_ref[t]], tiles_ref[t], NT)
        for i in range(row_tiles):
            totals[i] = totals[i] + jnp.where(rows_ref[t] == i, term, 0.0)
    for i in range(row_tiles):
        head, rest = halves(totals[i])
        cut = slice(i * LANES, (i + 1) * LANES)
        for n in range(out_ref.shape[0]):
            out_ref[n, 0:part, cut] = head
            out_ref[n, part : 2 * part, cut] = rest
    for n in range(out_ref.shape[0]):
        out_ref[n, 2 * part : 3 * part] = weight_ref[...]
        out_ref[n, 3 * part :] = cot_ref[...]


def middle_kernel(
    rows_ref, cols_ref, me_ref, tiles_ref, group_ref, weight_ref, norm_ref, act_ref, out_ref, pre_ref, total_ref
):
    part = weight_ref.shape[0]
    hid_part = act_ref.shape[0]
    n_feat = group_ref.shape[0]
    group = group_ref[...]
    head = group[:, 0:part].reshape(n_feat * part, -1)
    rest = group[:, part : 2 * part].reshape(n_feat * part, -1)
    weight_all = group[:, 2 * part : 3 * part].reshape(n_feat * part, -1)
    cot = group[:, 3 * part :].reshape(n_feat * hid_part, -1)
    norm = norm_ref[...]
    pre = (dot(weight_all, head, TN) + dot(weight_all, rest, TN)) * norm
    pre_ref[...] = pre
    sigma = 1.0 / (1.0 + jnp.exp(-pre))
    slope = sigma * (1.0 + pre * (1.0 - sigma))
    back_in = (cot.astype(F32) * slope * norm).astype(BF16)
    own = pre_ref[pl.ds(pl.multiple_of(me_ref[0] * hid_part, hid_part), hid_part)]
    act_ref[...] = (own / (1.0 + jnp.exp(-own))).astype(BF16)

    back = dot(weight_ref[...], back_in, NN)
    row_tiles = back.shape[1] // LANES
    back_head, back_rest = halves(back)
    back_tiles = [
        jnp.concatenate([h[:, i * LANES : (i + 1) * LANES] for h in (back_head, back_rest)], axis=0)
        for i in range(row_tiles)
    ]
    total_ref[...] = jnp.zeros_like(total_ref)
    for t in range(tiles_ref.shape[0]):
        left = back_tiles[0]
        for i in range(1, row_tiles):
            left = jnp.where(rows_ref[t] == i, back_tiles[i], left)
        both = dot(left, tiles_ref[t], NN)
        total_ref[cols_ref[t]] += both[:part] + both[part:]

    own_head = group_ref[pl.ds(me_ref[0], 1), 0:part][0]
    own_rest = group_ref[pl.ds(me_ref[0], 1), part : 2 * part][0]
    weight_part = dot(own_head, back_in, NT) + dot(own_rest, back_in, NT)
    n_first, n_rows, _ = out_ref.shape
    cols = total_ref.shape[0] // n_first
    total = total_ref[...].astype(BF16).reshape(n_first, cols * part, LANES)
    out_ref[:, : cols * part] = total
    sent = halves(weight_part)
    spot = cols * part
    for value in sent:
        for j in range(value.shape[1] // LANES):
            piece = value[:, j * LANES : (j + 1) * LANES]
            for n in range(n_first):
                out_ref[n, spot : spot + part] = piece
            spot += part


def relay_kernel(got_ref, out_ref, *, own):
    n_peer = out_ref.shape[0]
    total = got_ref[0].astype(F32)
    for n in range(1, got_ref.shape[0]):
        total = total + got_ref[n].astype(F32)
    out_ref[:, :own] = total[: n_peer * own].astype(BF16).reshape(n_peer, own, LANES)
    value = total[n_peer * own :]
    half = value.shape[0] // 2
    head, rest = halves(value[:half] + value[half:])
    for n in range(n_peer):
        out_ref[n, own : own + half] = head
        out_ref[n, own + half :] = rest


def end_kernel(got_ref, norm_ref, grad_ref, weight_ref):
    total = got_ref[0].astype(F32)
    for n in range(1, got_ref.shape[0]):
        total = total + got_ref[n].astype(F32)
    part = grad_ref.shape[0]
    spot = 0
    for i in range(grad_ref.shape[1] // LANES):
        cut = slice(i * LANES, (i + 1) * LANES)
        grad_ref[:, cut] = (total[spot : spot + part] * norm_ref[:, cut]).astype(BF16)
        spot += part
    half = (total.shape[0] - spot) // 2
    for j in range(weight_ref.shape[1] // LANES):
        weight_ref[:, j * LANES : (j + 1) * LANES] = (
            total[spot : spot + part] + total[spot + half : spot + half + part]
        )
        spot += part


SMEM = pl.BlockSpec(memory_space=pltpu.SMEM)
VMEM = pl.BlockSpec(memory_space=pltpu.VMEM)
SCOPED = pltpu.CompilerParams(vmem_limit_bytes=24 * 2**20)


def call(kernel, outs, in_specs, *args, scratch=()):
    return pl.pallas_call(
        kernel,
        out_shape=outs,
        in_specs=in_specs,
        out_specs=jax.tree.map(lambda _: VMEM, outs),
        scratch_shapes=list(scratch),
        compiler_params=SCOPED,
    )(*args)


def per_device(features, weight, norm_scale, tile_rows, tile_cols, tile_vals, cotangent):
    rows_dev, part = features.shape
    tile_len = tile_vals.shape[1]
    row_tiles = rows_dev // tile_len
    hid_part = cotangent.shape[1]
    hidden = weight.shape[1]
    n_first = lax.axis_size(FIRST)
    n_second = lax.axis_size(SECOND)
    n_feat = lax.axis_size(FEAT)
    col_tiles = n_first * n_second * row_tiles
    norm = norm_scale.reshape(1, rows_dev)
    n_z = lax.axis_size("z")
    tile, owner = tile_cols % row_tiles, tile_cols // row_tiles
    owner_z, owner_y = owner % n_z, owner // n_z % n_second
    owner_x = owner // (n_z * n_second)
    spots = ((owner_x * n_z + owner_z) * n_second + owner_y) * row_tiles + tile
    me = lax.axis_index(FEAT).reshape(1).astype(jnp.int32)
    shape = jax.ShapeDtypeStruct

    block = call(
        start_kernel,
        shape((n_second, row_tiles, part, tile_len), BF16),
        [VMEM, VMEM],
        features.T,
        norm,
    )
    block = lax.all_to_all(block, SECOND, 0, 0)
    block = lax.all_to_all(
        jnp.broadcast_to(block[None], (n_first,) + block.shape), FIRST, 0, 0
    )
    group = call(
        forward_kernel,
        shape((n_feat, 3 * part + hid_part, rows_dev), BF16),
        [SMEM, SMEM, VMEM, VMEM, VMEM, VMEM],
        tile_rows,
        spots,
        tile_vals,
        block.reshape(col_tiles, part, tile_len),
        weight,
        cotangent.T,
    )
    group = lax.all_to_all(group, FEAT, 0, 0)
    own = row_tiles * part
    weight_rows = 2 * part * hidden // tile_len
    activated, sent = call(
        middle_kernel,
        (
            shape((hid_part, rows_dev), BF16),
            shape((n_first, n_second * own + weight_rows, tile_len), BF16),
        ),
        [SMEM, SMEM, SMEM, VMEM, VMEM, VMEM, VMEM],
        tile_rows,
        spots,
        me,
        tile_vals,
        group,
        weight,
        norm,
        scratch=(
            pltpu.VMEM((hidden, rows_dev), F32),
            pltpu.VMEM((col_tiles, part, tile_len), F32),
        ),
    )
    got = lax.all_to_all(sent, FIRST, 0, 0)
    sent = call(
        functools.partial(relay_kernel, own=own),
        shape((n_second, own + weight_rows, tile_len), BF16),
        [VMEM],
        got,
    )
    got = lax.all_to_all(sent, SECOND, 0, 0)
    feature_grad, weight_grad = call(
        end_kernel,
        (shape((part, rows_dev), BF16), shape((part, hidden), F32)),
        [VMEM, VMEM],
        got,
        norm,
    )
    return (activated.T, weight_grad, feature_grad.T)


FIRST, SECOND, FEAT = ("x", "z"), "y", "feat"


def axes_of(rows):
    return (4, 8, 3) if rows == 96 else (2, rows // 4, 2)


def solution(mesh):
    fine = Mesh(
        mesh.devices.reshape(axes_of(mesh.shape["row"]) + (mesh.shape["feat"],)), ("x", "y", "z", "feat")
    )
    row = ("x", "y", "z")
    placed = (
        P(row, "feat"),
        P("feat", None),
        P(row),
        P(row),
        P(row),
        P(row, None, None),
        P(row, "feat"),
    )
    return jax.shard_map(
        per_device,
        mesh=fine,
        in_specs=placed,
        out_specs=(P(row, "feat"), P("feat", None), P(row, "feat")),
        check_vma=False,
    )
```

time: 1720 us -> 111 us (0.06)
  waiting for transfers between devices: 1040 us -> 32.1 us
  blocking collectives: 574 us -> 51.3 us
  other arithmetic: 45 us -> 0.03 us
  local copies, waits for them, and re-layouts: 38.8 us -> 2.54 us
  starting transfers between devices: 0.12 us -> 19.1 us
    reduce_scatter x2 -> x0, waiting for transfers between devices: 625 us -> none  [the longest x1 576 us: per_device(): lax.psum_scatter(jax.ops.segment_sum(kept, jnp.clip(offset, 0, rows_dev *...]
    psum x1 -> x0, blocking collectives: 558 us -> none  [per_device(): weight_grad = lax.psum(weight_part, 'row')]
    all_gather x1 -> x0, waiting for transfers between devices: 416 us -> none  [per_device(): rows_piece = lax.all_gather(source, 'row', axis=0, tiled=True)]
    all_to_all x0 -> x3, blocking collectives: none -> 51.3 us  [the longest x1 23.7 us: per_device(): got = lax.all_to_all(sent, FIRST, 0, 0)]
    scatter-add x1 -> x0, other arithmetic: 38.8 us -> none  [per_device(): jax.ops.segment_sum(kept, jnp.clip(offset, 0, rows_dev * lax.axis_size('r...]
    all_to_all x0 -> x2, waiting for transfers between devices: none -> 32.1 us  [the longest x1 16.1 us: per_device(): group = lax.all_to_all(group, FEAT, 0, 0)]
    gather x3 -> x0, local copies, waits for them, and re-layouts: 21.5 us -> none  [the longest x2 20.7 us: per_device(): fetched = rows_piece[jnp.clip(offset, 0, piece_len - 1)]]
    all_to_all x0 -> x2, starting transfers between devices: none -> 19.1 us  [the longest x1 9.89 us: per_device(): group = lax.all_to_all(group, FEAT, 0, 0)]
  transfers between devices with their start and end apart: 3 -> 2, of which waited for: 3 -> 2; matrix products, arithmetic and copies ran while one was open for 0% -> 0% of each run, Pallas kernels for 0% -> 0%
where the time goes in v2:
time: 111 us
  blocking collectives  51.3 us (46%)
  waiting for transfers between devices  32.1 us (29%)
  starting transfers between devices  19.1 us (17%)
  Pallas kernels  5.17 us (5%)
  local copies, waits for them, and re-layouts  2.54 us (2%)
    all_to_all x1, blocking collectives, per_device(): got = lax.all_to_all(sent, FIRST, 0, 0)  23.7 us
    all_to_all x1, waiting for transfers between devices, per_device(): group = lax.all_to_all(group, FEAT, 0, 0)  16.1 us
    all_to_all x1, waiting for transfers between devices, per_device(): lax.all_to_all(jnp.broadcast_to(block[None], (n_first,) + block.shape), F...  15.9 us
    all_to_all x1, blocking collectives, per_device(): block = lax.all_to_all(block, SECOND, 0, 0)  15.4 us
    all_to_all x1, blocking collectives, per_device(): got = lax.all_to_all(sent, SECOND, 0, 0)  12.2 us
    all_to_all x1, starting transfers between devices, per_device(): group = lax.all_to_all(group, FEAT, 0, 0)  9.89 us
    all_to_all x1, starting transfers between devices, per_device(): lax.all_to_all(jnp.broadcast_to(block[None], (n_first,) + block.shape), F...  9.16 us
    pallas_call x5, Pallas kernels, call(): pl.pallas_call(kernel, out_shape=outs, in_specs=in_specs, out_specs=jax.t...  5.17 us
  transfers between devices with their start and end apart: 2, of which 2 were waited for; matrix products, arithmetic and copies ran while one was open for 0% of the time, Pallas kernels for 0%

profile of v2, /device:TPU:192, one launch (start us, length us, event | category | flops | bytes accessed | tf_op | source)
XLA Modules:
  0.0 110.9 jit_solution(254946222019544937)
XLA Ops:
  0.6 0.0 copy-start
  0.6 0.0 copy-start.1
  0.7 0.0 copy-start.2
  0.7 0.0 copy-start.3
  0.7 0.8 copy-done.3
  1.5 0.0 copy-start.5
  1.5 0.7 copy-done.5
  2.2 0.0 copy-start.7
  2.2 0.0 copy-start.6
  2.2 15.4 %all_to_all.25 = bf16[8,2,16,128]{3,2,1,0:T(8,128)(2,1)S(1)} all-to-all(bf16[8,2,16,128]{3,2,1,0:T(8,128)(2,1)S(1)} %shard_map.94), channel_id=1, replica_groups=mesh['x'=4,'y'=8,'z'=3,'feat'=8] {'y'}, dimensions={0} | all-to-all | bytes 131072 | tf_op jit(solution)/shard_map/all_to_all | solution.py:179
  17.6 1.0 broadcast_in_dim.2
  18.6 9.2 %all-to-all-start.1 = ((bf16[12,8,2,16,128]{4,3,2,1,0:T(8,128)(2,1)}), bf16[12,8,2,16,128]{4,3,2,1,0:T(8,128)(2,1)S(1)}, u32[]{:S(2)}, u32[]{:S(2)}) async-start(bf16[12,8,2,16,128]{4,3,2,1,0:T(8,128)(2,1)} %broadcast_in_dim.2), calls=%async_computation.1 | async-start | bytes 1572864 | tf_op jit(solution)/shard_map/all_to_all | solution.py:180
  27.8 0.0 copy-done.7
  27.8 15.9 %all-to-all-done.1 = bf16[12,8,2,16,128]{4,3,2,1,0:T(8,128)(2,1)S(1)} async-done(((bf16[12,8,2,16,128]{4,3,2,1,0:T(8,128)(2,1)}), bf16[12,8,2,16,128]{4,3,2,1,0:T(8,128)(2,1)S(1)}, u32[]{:S(2)}, u32[]{:S(2)}) %all-to-all-start.1) | async-done | bytes 786464 | tf_op jit(solution)/shard_map/all_to_all | solution.py:180
  43.8 0.0 copy-done
  43.8 0.0 copy-done.1
  43.8 0.0 copy-done.2
  43.8 0.0 copy-done.6
  43.8 0.0 copy-start.4
  43.8 2.2 %shard_map.95 = bf16[8,80,256]{2,1,0:T(8,128)(2,1)} custom-call(s32[48]{0:T(128)S(1)} %copy-done.6, s32[48]{0:T(128)S(1)} %fusion.2.cols_ref, bf16[48,128,128]{2,1,0:T(8,128)(2,1)S(1)} %copy-done, bf16[192,16,128]{2,1,0:T(8,128)(2,1)S(1)} %bitcast.7, bf16[16,256]{1,0:T(8,128)(2,1)S(1)} %copy-done.1, bf16[32,256]{1,0:T(8,128)(2,1)S(1)} %bitcast.8), custom_call_target="tpu_custom_call" | custom-call | tf_op jit(solution)/shard_map/pallas_call | solution.py:143
  46.0 9.9 %all-to-all-start.2 = ((bf16[8,80,256]{2,1,0:T(8,128)(2,1)}), bf16[8,80,256]{2,1,0:T(8,128)(2,1)S(1)}, u32[]{:S(2)}, u32[]{:S(2)}) async-start(bf16[8,80,256]{2,1,0:T(8,128)(2,1)} %shard_map.95), calls=%async_computation.2 | async-start | bytes 655360 | tf_op jit(solution)/shard_map/all_to_all | solution.py:194
  55.9 16.1 %all-to-all-done.2.group_ref = bf16[8,80,256]{2,1,0:T(8,128)(2,1)S(1)} async-done(((bf16[8,80,256]{2,1,0:T(8,128)(2,1)}), bf16[8,80,256]{2,1,0:T(8,128)(2,1)S(1)}, u32[]{:S(2)}, u32[]{:S(2)}) %all-to-all-start.2) | async-done | bytes 327712 | tf_op jit(solution)/shard_map/all_to_all | solution.py:194
  72.0 0.0 copy-done.4
  72.0 2.2 %shard_map.96 = (bf16[32,256]{1,0:T(8,128)(2,1)}, bf16[12,320,128]{2,1,0:T(8,128)(2,1)S(1)}) custom-call(s32[48]{0:T(128)S(1)} %copy-done.6, s32[48]{0:T(128)S(1)} %fusion.2.cols_ref, s32[1]{0:T(128)} %bitcast.me_ref, bf16[48,128,128]{2,1,0:T(8,128)(2,1)S(1)} %copy-done, bf16[8,80,256]{2,1,0:T(8,128)(2,1)S(1)} %all-to-all-done.2.group_ref, ...), custom_call_target="tpu_custom_call" | custom-call | tf_op jit(solution)/shard_map/pallas_call | solution.py:143
  74.2 23.7 %all_to_all.26.got_ref = bf16[12,320,128]{2,1,0:T(8,128)(2,1)S(1)} all-to-all(bf16[12,320,128]{2,1,0:T(8,128)(2,1)S(1)} %get-tuple-element.8), channel_id=1, replica_groups=mesh['x'=4,'y'=8,'z'=3,'feat'=8] {'x','z'}, dimensions={0} | all-to-all | bytes 1966080 | tf_op jit(solution)/shard_map/all_to_all | solution.py:216
  97.9 0.1 shard_map.97
  98.1 12.2 %all_to_all.27.got_ref = bf16[8,96,128]{2,1,0:T(8,128)(2,1)S(1)} all-to-all(bf16[8,96,128]{2,1,0:T(8,128)(2,1)S(1)} %shard_map.97), channel_id=1, replica_groups=mesh['x'=4,'y'=8,'z'=3,'feat'=8] {'y'}, dimensions={0} | all-to-all | bytes 393216 | tf_op jit(solution)/shard_map/all_to_all | solution.py:223
  110.3 0.6 shard_map.98
  (2 shorter events, 0.0 us)
Async XLA Ops:
  0.6 43.1 %copy-start = (bf16[48,128,128]{2,1,0:T(8,128)(2,1)S(1)}, bf16[48,128,128]{2,1,0:T(8,128)(2,1)}, u32[]{:S(2)}) copy-start(bf16[48,128,128]{2,1,0:T(8,128)(2,1)} %tiles_ref.3) | copy-start | bytes 4718596
  0.6 43.1 %copy-start.1 = (bf16[16,256]{1,0:T(8,128)(2,1)S(1)}, bf16[16,256]{1,0:T(8,128)(2,1)}, u32[]{:S(2)}) copy-start(bf16[16,256]{1,0:T(8,128)(2,1)} %weight_ref.3) | copy-start | bytes 24580
  0.7 43.1 %copy-start.2 = (bf16[256,32]{0,1:T(8,128)(2,1)S(1)}, bf16[256,32]{0,1:T(8,128)(2,1)}, u32[]{:S(2)}) copy-start(bf16[256,32]{0,1:T(8,128)(2,1)} %param.13) | copy-start | bytes 49156
  0.7 0.8 copy-start.3
  1.5 0.7 copy-start.5
  2.2 25.6 %copy-start.7 = (s32[48]{0:T(128)S(1)}, s32[48]{0:T(128)}, u32[]{:S(2)}) copy-start(s32[48]{0:T(128)} %param.11) | copy-start | bytes 580
  2.2 41.6 %copy-start.6 = (s32[48]{0:T(128)S(1)}, s32[48]{0:T(128)}, u32[]{:S(2)}) copy-start(s32[48]{0:T(128)} %rows_ref.3) | copy-start | bytes 580
  18.6 25.2 %all-to-all-start.1 = ((bf16[12,8,2,16,128]{4,3,2,1,0:T(8,128)(2,1)}), bf16[12,8,2,16,128]{4,3,2,1,0:T(8,128)(2,1)S(1)}, u32[]{:S(2)}, u32[]{:S(2)}) async-start(bf16[12,8,2,16,128]{4,3,2,1,0:T(8,128)(2,1)} %broadcast_in_dim.2), calls=%async_computation.1 | async-start | bytes 1572864 | tf_op jit(solution)/shard_map/all_to_all | solution.py:180
  43.8 28.2 %copy-start.4 = (f32[256]{0:T(256)S(1)}, f32[256]{0:T(256)}, u32[]{:S(2)}) copy-start(f32[256]{0:T(256)} %param.9) | copy-start | bytes 3076
  46.0 26.0 %all-to-all-start.2 = ((bf16[8,80,256]{2,1,0:T(8,128)(2,1)}), bf16[8,80,256]{2,1,0:T(8,128)(2,1)S(1)}, u32[]{:S(2)}, u32[]{:S(2)}) async-start(bf16[8,80,256]{2,1,0:T(8,128)(2,1)} %shard_map.95), calls=%async_computation.2 | async-start | bytes 655360 | tf_op jit(solution)/shard_map/all_to_all | solution.py:194

commit v3 on v2

--- a/solution.py
+++ b/solution.py
@@ -31,12 +31,20 @@
             out_ref[n, i] = scaled[:, i * LANES : (i + 1) * LANES]
 
 
+def spot_of(tile, row_tiles):
+    n_z, n_y = lax.axis_size("z"), lax.axis_size("y")
+    within, owner = lax.rem(tile, row_tiles), lax.div(tile, row_tiles)
+    z, owner = lax.rem(owner, n_z), lax.div(owner, n_z)
+    y, x = lax.rem(owner, n_y), lax.div(owner, n_y)
+    return ((x * n_z + z) * n_y + y) * row_tiles + within
+
+
 def forward_kernel(rows_ref, cols_ref, tiles_ref, nodes_ref, weight_ref, cot_ref, out_ref):
     part = weight_ref.shape[0]
     row_tiles = cot_ref.shape[1] // LANES
     totals = [jnp.zeros((part, LANES), F32) for _ in range(row_tiles)]
     for t in range(tiles_ref.shape[0]):
-        term = dot(nodes_ref[cols_ref[t]], tiles_ref[t], NT)
+        term = dot(nodes_ref[spot_of(cols_ref[t], row_tiles)], tiles_ref[t], NT)
         for i in range(row_tiles):
             totals[i] = totals[i] + jnp.where(rows_ref[t] == i, term, 0.0)
     for i in range(row_tiles):
@@ -51,8 +59,9 @@
 
 
 def middle_kernel(
-    rows_ref, cols_ref, me_ref, tiles_ref, group_ref, weight_ref, norm_ref, act_ref, out_ref, pre_ref, total_ref
+    rows_ref, cols_ref, tiles_ref, group_ref, weight_ref, norm_ref, act_ref, out_ref, pre_ref, total_ref
 ):
+    me = lax.axis_index(FEAT)
     part = weight_ref.shape[0]
     hid_part = act_ref.shape[0]
     n_feat = group_ref.shape[0]
@@ -67,7 +76,7 @@
     sigma = 1.0 / (1.0 + jnp.exp(-pre))
     slope = sigma * (1.0 + pre * (1.0 - sigma))
     back_in = (cot.astype(F32) * slope * norm).astype(BF16)
-    own = pre_ref[pl.ds(pl.multiple_of(me_ref[0] * hid_part, hid_part), hid_part)]
+    own = pre_ref[pl.ds(pl.multiple_of(me * hid_part, hid_part), hid_part)]
     act_ref[...] = (own / (1.0 + jnp.exp(-own))).astype(BF16)
 
     back = dot(weight_ref[...], back_in, NN)
@@ -83,10 +92,10 @@
         for i in range(1, row_tiles):
             left = jnp.where(rows_ref[t] == i, back_tiles[i], left)
         both = dot(left, tiles_ref[t], NN)
-        total_ref[cols_ref[t]] += both[:part] + both[part:]
-
-    own_head = group_ref[pl.ds(me_ref[0], 1), 0:part][0]
-    own_rest = group_ref[pl.ds(me_ref[0], 1), part : 2 * part][0]
+        total_ref[spot_of(cols_ref[t], row_tiles)] += both[:part] + both[part:]
+
+    own_head = group_ref[pl.ds(me, 1), 0:part][0]
+    own_rest = group_ref[pl.ds(me, 1), part : 2 * part][0]
     weight_part = dot(own_head, back_in, NT) + dot(own_rest, back_in, NT)
     n_first, n_rows, _ = out_ref.shape
     cols = total_ref.shape[0] // n_first
@@ -161,12 +170,6 @@
     n_feat = lax.axis_size(FEAT)
     col_tiles = n_first * n_second * row_tiles
     norm = norm_scale.reshape(1, rows_dev)
-    n_z = lax.axis_size("z")
-    tile, owner = tile_cols % row_tiles, tile_cols // row_tiles
-    owner_z, owner_y = owner % n_z, owner // n_z % n_second
-    owner_x = owner // (n_z * n_second)
-    spots = ((owner_x * n_z + owner_z) * n_second + owner_y) * row_tiles + tile
-    me = lax.axis_index(FEAT).reshape(1).astype(jnp.int32)
     shape = jax.ShapeDtypeStruct
 
     block = call(
@@ -185,7 +188,7 @@
         shape((n_feat, 3 * part + hid_part, rows_dev), BF16),
         [SMEM, SMEM, VMEM, VMEM, VMEM, VMEM],
         tile_rows,
-        spots,
+        tile_cols,
         tile_vals,
         block.reshape(col_tiles, part, tile_len),
         weight,
@@ -200,10 +203,9 @@
             shape((hid_part, rows_dev), BF16),
             shape((n_first, n_second * own + weight_rows, tile_len), BF16),
         ),
-        [SMEM, SMEM, SMEM, VMEM, VMEM, VMEM, VMEM],
+        [SMEM, SMEM, VMEM, VMEM, VMEM, VMEM],
         tile_rows,
-        spots,
-        me,
+        tile_cols,
         tile_vals,
         group,
         weight,

time: 111 us -> 111 us (level)
  the two profiles are of different devices: /device:TPU:192 before, /device:TPU:1 now
where the time goes in v3:
time: 111 us; the launch traced here: 110 us
  blocking collectives  103 us (93%)
  Pallas kernels  4.53 us (4%)
  local copies, waits for them, and re-layouts  1.64 us (1%)
    all_to_all x1, blocking collectives, per_device(): group = lax.all_to_all(group, FEAT, 0, 0)  34.2 us
    all_to_all x1, blocking collectives, per_device(): got = lax.all_to_all(sent, FIRST, 0, 0)  21.9 us
    all_to_all x1, blocking collectives, per_device(): lax.all_to_all(jnp.broadcast_to(block[None], (n_first,) + block.shape), F...  21.3 us
    all_to_all x1, blocking collectives, per_device(): block = lax.all_to_all(block, SECOND, 0, 0)  14.8 us
    all_to_all x1, blocking collectives, per_device(): got = lax.all_to_all(sent, SECOND, 0, 0)  11.1 us
    pallas_call x5, Pallas kernels, call(): pl.pallas_call(kernel, out_shape=outs, in_specs=in_specs, out_specs=jax.t...  4.53 us

profile of v3, /device:TPU:1, one launch (start us, length us, event | category | flops | bytes accessed | tf_op | source)
XLA Modules:
  0.0 110.1 jit_solution(11207649719892883649)
XLA Ops:
  0.6 0.0 copy-start
  0.6 0.0 copy-start.1
  0.7 0.0 copy-start.2
  0.7 0.0 copy-start.3
  0.7 0.8 copy-done.3
  1.5 0.0 copy-start.5
  1.5 0.7 copy-done.5
  2.2 0.0 copy-start.6
  2.2 0.0 copy-start.7
  2.2 14.8 %all_to_all.25 = bf16[8,2,16,128]{3,2,1,0:T(8,128)(2,1)S(1)} all-to-all(bf16[8,2,16,128]{3,2,1,0:T(8,128)(2,1)S(1)} %shard_map.94), channel_id=1, replica_groups=mesh['x'=4,'y'=8,'z'=3,'feat'=8] {'y'}, dimensions={0} | all-to-all | bytes 131072 | tf_op jit(solution)/shard_map/all_to_all | solution.py:182
  17.0 0.1 broadcast_in_dim.2
  17.1 21.3 %all_to_all.26 = bf16[12,8,2,16,128]{4,3,2,1,0:T(8,128)(2,1)S(1)} all-to-all(bf16[12,8,2,16,128]{4,3,2,1,0:T(8,128)(2,1)S(1)} %broadcast_in_dim.2), channel_id=1, replica_groups=mesh['x'=4,'y'=8,'z'=3,'feat'=8] {'x','z'}, dimensions={0} | all-to-all | bytes 1572864 | tf_op jit(solution)/shard_map/all_to_all | solution.py:183
  38.4 0.0 copy-done
  38.4 0.0 copy-done.1
  38.4 0.0 copy-done.2
  38.4 0.0 copy-done.6
  38.4 0.0 copy-done.7
  38.4 0.0 copy-start.4
  38.5 1.5 %shard_map.95 = bf16[8,80,256]{2,1,0:T(8,128)(2,1)S(1)} custom-call(s32[48]{0:T(128)S(1)} %copy-done.6, s32[48]{0:T(128)S(1)} %copy-done.7, bf16[48,128,128]{2,1,0:T(8,128)(2,1)S(1)} %copy-done, bf16[192,16,128]{2,1,0:T(8,128)(2,1)S(1)} %bitcast.6, bf16[16,256]{1,0:T(8,128)(2,1)S(1)} %copy-done.1, bf16[32,256]{1,0:T(8,128)(2,1)S(1)} %bitcast.7), custom_call_target="tpu_custom_call" | custom-call | tf_op jit(solution)/shard_map/pallas_call | solution.py:152
  40.0 34.2 %all_to_all.27.group_ref = bf16[8,80,256]{2,1,0:T(8,128)(2,1)S(1)} all-to-all(bf16[8,80,256]{2,1,0:T(8,128)(2,1)S(1)} %shard_map.95), channel_id=1, replica_groups=mesh['x'=4,'y'=8,'z'=3,'feat'=8] {'feat'}, dimensions={0} | all-to-all | bytes 655360 | tf_op jit(solution)/shard_map/all_to_all | solution.py:197
  74.1 0.0 copy-done.4
  74.1 2.3 %shard_map.96 = (bf16[32,256]{1,0:T(8,128)(2,1)}, bf16[12,320,128]{2,1,0:T(8,128)(2,1)S(1)}) custom-call(s32[48]{0:T(128)S(1)} %copy-done.6, s32[48]{0:T(128)S(1)} %copy-done.7, bf16[48,128,128]{2,1,0:T(8,128)(2,1)S(1)} %copy-done, bf16[8,80,256]{2,1,0:T(8,128)(2,1)S(1)} %all_to_all.27.group_ref, bf16[16,256]{1,0:T(8,128)(2,1)S(1)} %copy-done.1, ...), custom_call_target="tpu_custom_call" | custom-call | tf_op jit(solution)/shard_map/pallas_call | solution.py:152
  76.4 21.9 %all_to_all.28.got_ref = bf16[12,320,128]{2,1,0:T(8,128)(2,1)S(1)} all-to-all(bf16[12,320,128]{2,1,0:T(8,128)(2,1)S(1)} %get-tuple-element.8), channel_id=1, replica_groups=mesh['x'=4,'y'=8,'z'=3,'feat'=8] {'x','z'}, dimensions={0} | all-to-all | bytes 1966080 | tf_op jit(solution)/shard_map/all_to_all | solution.py:218
  98.3 0.1 shard_map.97
  98.4 11.1 %all_to_all.29.got_ref = bf16[8,96,128]{2,1,0:T(8,128)(2,1)S(1)} all-to-all(bf16[8,96,128]{2,1,0:T(8,128)(2,1)S(1)} %shard_map.97), channel_id=1, replica_groups=mesh['x'=4,'y'=8,'z'=3,'feat'=8] {'y'}, dimensions={0} | all-to-all | bytes 393216 | tf_op jit(solution)/shard_map/all_to_all | solution.py:225
  109.5 0.6 shard_map.98
  (1 shorter events, 0.0 us)
Async XLA Ops:
  0.6 37.8 %copy-start = (bf16[48,128,128]{2,1,0:T(8,128)(2,1)S(1)}, bf16[48,128,128]{2,1,0:T(8,128)(2,1)}, u32[]{:S(2)}) copy-start(bf16[48,128,128]{2,1,0:T(8,128)(2,1)} %tiles_ref.3) | copy-start | bytes 4718596
  0.6 37.8 %copy-start.1 = (bf16[16,256]{1,0:T(8,128)(2,1)S(1)}, bf16[16,256]{1,0:T(8,128)(2,1)}, u32[]{:S(2)}) copy-start(bf16[16,256]{1,0:T(8,128)(2,1)} %weight_ref.3) | copy-start | bytes 24580
  0.7 37.8 %copy-start.2 = (bf16[256,32]{0,1:T(8,128)(2,1)S(1)}, bf16[256,32]{0,1:T(8,128)(2,1)}, u32[]{:S(2)}) copy-start(bf16[256,32]{0,1:T(8,128)(2,1)} %param.13) | copy-start | bytes 49156
  0.7 0.8 copy-start.3
  1.5 0.7 copy-start.5
  2.2 36.3 %copy-start.6 = (s32[48]{0:T(128)S(1)}, s32[48]{0:T(128)}, u32[]{:S(2)}) copy-start(s32[48]{0:T(128)} %rows_ref.3) | copy-start | bytes 580
  2.2 36.3 %copy-start.7 = (s32[48]{0:T(128)S(1)}, s32[48]{0:T(128)}, u32[]{:S(2)}) copy-start(s32[48]{0:T(128)} %cols_ref.3) | copy-start | bytes 580
  38.4 35.7 %copy-start.4 = (f32[256]{0:T(256)S(1)}, f32[256]{0:T(256)}, u32[]{:S(2)}) copy-start(f32[256]{0:T(256)} %param.9) | copy-start | bytes 3076

commit v4 on v3

--- a/solution.py
+++ b/solution.py
@@ -24,19 +24,12 @@
     return lax.dot_general(left, right, dims, preferred_element_type=F32)
 
 
-def start_kernel(features_ref, norm_ref, out_ref):
-    scaled = (features_ref[...].astype(F32) * norm_ref[...]).astype(BF16)
-    for n in range(out_ref.shape[0]):
-        for i in range(out_ref.shape[1]):
-            out_ref[n, i] = scaled[:, i * LANES : (i + 1) * LANES]
-
-
 def spot_of(tile, row_tiles):
     n_z, n_y = lax.axis_size("z"), lax.axis_size("y")
     within, owner = lax.rem(tile, row_tiles), lax.div(tile, row_tiles)
     z, owner = lax.rem(owner, n_z), lax.div(owner, n_z)
     y, x = lax.rem(owner, n_y), lax.div(owner, n_y)
-    return ((x * n_z + z) * n_y + y) * row_tiles + within
+    return (x * n_z + z) * n_y + y, within
 
 
 def forward_kernel(rows_ref, cols_ref, tiles_ref, nodes_ref, weight_ref, cot_ref, out_ref):
@@ -44,7 +37,9 @@
     row_tiles = cot_ref.shape[1] // LANES
     totals = [jnp.zeros((part, LANES), F32) for _ in range(row_tiles)]
     for t in range(tiles_ref.shape[0]):
-        term = dot(nodes_ref[spot_of(cols_ref[t], row_tiles)], tiles_ref[t], NT)
+        owner, within = spot_of(cols_ref[t], row_tiles)
+        nodes = nodes_ref[owner, :, pl.ds(pl.multiple_of(within * LANES, LANES), LANES)]
+        term = dot(nodes, tiles_ref[t], NT)
         for i in range(row_tiles):
             totals[i] = totals[i] + jnp.where(rows_ref[t] == i, term, 0.0)
     for i in range(row_tiles):
@@ -61,7 +56,9 @@
 def middle_kernel(
     rows_ref, cols_ref, tiles_ref, group_ref, weight_ref, norm_ref, act_ref, out_ref, pre_ref, total_ref
 ):
-    me = lax.axis_index(FEAT)
+    my_zh, my_core = lax.axis_index("zh"), lax.axis_index("core")
+    n_zh, n_core = lax.axis_size("zh"), lax.axis_size("core")
+    me, my_place = my_zh * n_core + my_core, my_core * n_zh + my_zh
     part = weight_ref.shape[0]
     hid_part = act_ref.shape[0]
     n_feat = group_ref.shape[0]
@@ -69,7 +66,9 @@
     head = group[:, 0:part].reshape(n_feat * part, -1)
     rest = group[:, part : 2 * part].reshape(n_feat * part, -1)
     weight_all = group[:, 2 * part : 3 * part].reshape(n_feat * part, -1)
-    cot = group[:, 3 * part :].reshape(n_feat * hid_part, -1)
+    cot = jnp.concatenate(
+        [group[core * n_zh + zh, 3 * part :] for zh in range(n_zh) for core in range(n_core)], axis=0
+    )
     norm = norm_ref[...]
     pre = (dot(weight_all, head, TN) + dot(weight_all, rest, TN)) * norm
     pre_ref[...] = pre
@@ -92,23 +91,22 @@
         for i in range(1, row_tiles):
             left = jnp.where(rows_ref[t] == i, back_tiles[i], left)
         both = dot(left, tiles_ref[t], NN)
-        total_ref[spot_of(cols_ref[t], row_tiles)] += both[:part] + both[part:]
-
-    own_head = group_ref[pl.ds(me, 1), 0:part][0]
-    own_rest = group_ref[pl.ds(me, 1), part : 2 * part][0]
+        owner, within = spot_of(cols_ref[t], row_tiles)
+        total_ref[owner * row_tiles + within] += both[:part] + both[part:]
+
+    own_head = group_ref[pl.ds(my_place, 1), 0:part][0]
+    own_rest = group_ref[pl.ds(my_place, 1), part : 2 * part][0]
     weight_part = dot(own_head, back_in, NT) + dot(own_rest, back_in, NT)
     n_first, n_rows, _ = out_ref.shape
     cols = total_ref.shape[0] // n_first
     total = total_ref[...].astype(BF16).reshape(n_first, cols * part, LANES)
     out_ref[:, : cols * part] = total
-    sent = halves(weight_part)
+    weight_part = weight_part.astype(BF16)
     spot = cols * part
-    for value in sent:
-        for j in range(value.shape[1] // LANES):
-            piece = value[:, j * LANES : (j + 1) * LANES]
-            for n in range(n_first):
-                out_ref[n, spot : spot + part] = piece
-            spot += part
+    for j in range(weight_part.shape[1] // LANES):
+        for n in range(n_first):
+            out_ref[n, spot : spot + part] = weight_part[:, j * LANES : (j + 1) * LANES]
+        spot += part
 
 
 def relay_kernel(got_ref, out_ref, *, own):
@@ -117,12 +115,8 @@
     for n in range(1, got_ref.shape[0]):
         total = total + got_ref[n].astype(F32)
     out_ref[:, :own] = total[: n_peer * own].astype(BF16).reshape(n_peer, own, LANES)
-    value = total[n_peer * own :]
-    half = value.shape[0] // 2
-    head, rest = halves(value[:half] + value[half:])
     for n in range(n_peer):
-        out_ref[n, own : own + half] = head
-        out_ref[n, own + half :] = rest
+        out_ref[n, own:] = total[n_peer * own :].astype(BF16)
 
 
 def end_kernel(got_ref, norm_ref, grad_ref, weight_ref):
@@ -135,11 +129,8 @@
         cut = slice(i * LANES, (i + 1) * LANES)
         grad_ref[:, cut] = (total[spot : spot + part] * norm_ref[:, cut]).astype(BF16)
         spot += part
-    half = (total.shape[0] - spot) // 2
     for j in range(weight_ref.shape[1] // LANES):
-        weight_ref[:, j * LANES : (j + 1) * LANES] = (
-            total[spot : spot + part] + total[spot + half : spot + half + part]
-        )
+        weight_ref[:, j * LANES : (j + 1) * LANES] = total[spot : spot + part]
         spot += part
 
 
@@ -167,36 +158,30 @@
     hidden = weight.shape[1]
     n_first = lax.axis_size(FIRST)
     n_second = lax.axis_size(SECOND)
-    n_feat = lax.axis_size(FEAT)
     col_tiles = n_first * n_second * row_tiles
     norm = norm_scale.reshape(1, rows_dev)
     shape = jax.ShapeDtypeStruct
 
-    block = call(
-        start_kernel,
-        shape((n_second, row_tiles, part, tile_len), BF16),
-        [VMEM, VMEM],
-        features.T,
-        norm,
-    )
+    block = (features.T.astype(F32) * norm_scale[None, :]).astype(BF16)
+    block = jnp.broadcast_to(block[None], (n_second,) + block.shape)
     block = lax.all_to_all(block, SECOND, 0, 0)
     block = lax.all_to_all(
         jnp.broadcast_to(block[None], (n_first,) + block.shape), FIRST, 0, 0
     )
     group = call(
         forward_kernel,
-        shape((n_feat, 3 * part + hid_part, rows_dev), BF16),
+        shape((lax.axis_size("zh"), 3 * part + hid_part, rows_dev), BF16),
         [SMEM, SMEM, VMEM, VMEM, VMEM, VMEM],
         tile_rows,
         tile_cols,
         tile_vals,
-        block.reshape(col_tiles, part, tile_len),
+        block.reshape(n_first * n_second, part, rows_dev),
         weight,
         cotangent.T,
     )
-    group = lax.all_to_all(group, FEAT, 0, 0)
+    group = lax.all_gather(lax.all_to_all(group, "zh", 0, 0), "core", axis=0, tiled=True)
     own = row_tiles * part
-    weight_rows = 2 * part * hidden // tile_len
+    weight_rows = part * hidden // tile_len
     activated, sent = call(
         middle_kernel,
         (
@@ -233,31 +218,30 @@
     return (activated.T, weight_grad, feature_grad.T)
 
 
-FIRST, SECOND, FEAT = ("x", "z"), "y", "feat"
-
-
-def axes_of(rows):
-    return (4, 8, 3) if rows == 96 else (2, rows // 4, 2)
+FIRST, SECOND = ("x", "z"), "y"
+
+
+def axes_of(rows, feats):
+    return ((4, 8, 3) if rows == 96 else (2, rows // 4, 2)) + (feats // 2, 2)
 
 
 def solution(mesh):
-    fine = Mesh(
-        mesh.devices.reshape(axes_of(mesh.shape["row"]) + (mesh.shape["feat"],)), ("x", "y", "z", "feat")
-    )
-    row = ("x", "y", "z")
+    sizes = axes_of(mesh.shape["row"], mesh.shape["feat"])
+    fine = Mesh(mesh.devices.reshape(sizes), ("x", "y", "z", "zh", "core"))
+    row, feat = ("x", "y", "z"), ("zh", "core")
     placed = (
-        P(row, "feat"),
-        P("feat", None),
+        P(row, feat),
+        P(feat, None),
         P(row),
         P(row),
         P(row),
         P(row, None, None),
-        P(row, "feat"),
+        P(row, feat),
     )
     return jax.shard_map(
         per_device,
         mesh=fine,
         in_specs=placed,
-        out_specs=(P(row, "feat"), P("feat", None), P(row, "feat")),
+        out_specs=(P(row, feat), P(feat, None), P(row, feat)),
         check_vma=False,
     )

time: 111 us -> 104 us (0.937)
  blocking collectives: 103 us -> 97.1 us
  local copies, waits for them, and re-layouts: 1.64 us -> 0.1 us
    all_to_all x1, blocking collectives: 34.2 us -> 23.9 us  [per_device(): lax.all_to_all(group, 'zh', 0, 0)]
    all_gather x0 -> x1, blocking collectives: none -> 6.65 us  [per_device(): lax.all_gather(lax.all_to_all(group, 'zh', 0, 0), 'core', axis=0, tiled=T...]
    all_to_all x1, blocking collectives: 21.9 us -> 20.1 us  [per_device(): got = lax.all_to_all(sent, FIRST, 0, 0)]
    unnamed x16 -> x12, local copies, waits for them, and re-layouts: 1.51 us -> 0.03 us
    pallas_call x5 -> x4, Pallas kernels: 4.53 us -> 4.48 us  [call(): pl.pallas_call(kernel, out_shape=outs, in_specs=in_specs, out_specs=jax.t...]
where the time goes in v4:
time: 104 us; the launch traced here: 103 us
  blocking collectives  97.1 us (93%)
  Pallas kernels  4.48 us (4%)
    all_to_all x1, blocking collectives, per_device(): lax.all_to_all(group, 'zh', 0, 0)  23.9 us
    all_to_all x1, blocking collectives, per_device(): lax.all_to_all(jnp.broadcast_to(block[None], (n_first,) + block.shape), F...  21.3 us
    all_to_all x1, blocking collectives, per_device(): got = lax.all_to_all(sent, FIRST, 0, 0)  20.1 us
    all_to_all x1, blocking collectives, per_device(): block = lax.all_to_all(block, SECOND, 0, 0)  14.7 us
    all_to_all x1, blocking collectives, per_device(): got = lax.all_to_all(sent, SECOND, 0, 0)  10.3 us
    all_gather x1, blocking collectives, per_device(): lax.all_gather(lax.all_to_all(group, 'zh', 0, 0), 'core', axis=0, tiled=T...  6.65 us
    pallas_call x4, Pallas kernels, call(): pl.pallas_call(kernel, out_shape=outs, in_specs=in_specs, out_specs=jax.t...  4.48 us

profile of v4, /device:TPU:1, one launch (start us, length us, event | category | flops | bytes accessed | tf_op | source)
XLA Modules:
  0.0 103.2 jit_solution(2549043168056958782)
XLA Ops:
  0.6 0.0 copy-start
  0.6 0.0 copy-start.5
  0.7 0.0 copy-start.4
  0.7 0.0 copy-start.1
  0.7 0.0 copy-start.2
  0.7 0.8 fusion
  1.5 14.7 %all_to_all.25 = bf16[8,16,256]{2,1,0:T(8,128)(2,1)S(1)} all-to-all(bf16[8,16,256]{2,1,0:T(8,128)(2,1)S(1)} %broadcast_in_dim.6), channel_id=1, replica_groups=mesh['x'=4,'y'=8,'z'=3,'zh'=4,'core'=2] {'y'}, dimensions={0} | all-to-all | bytes 131072 | tf_op jit(solution)/shard_map/all_to_all | solution.py:167
  16.2 0.1 broadcast_in_dim.7
  16.3 21.3 %all_to_all.26 = bf16[12,8,16,256]{3,2,1,0:T(8,128)(2,1)S(1)} all-to-all(bf16[12,8,16,256]{3,2,1,0:T(8,128)(2,1)S(1)} %broadcast_in_dim.7), channel_id=1, replica_groups=mesh['x'=4,'y'=8,'z'=3,'zh'=4,'core'=2] {'x','z'}, dimensions={0} | all-to-all | bytes 1572864 | tf_op jit(solution)/shard_map/all_to_all | solution.py:168
  37.5 0.0 copy-done
  37.6 0.0 copy-done.5
  37.6 0.0 copy-done.4
  37.6 0.0 copy-done.1
  37.6 0.0 copy-done.2
  37.6 0.0 copy-start.3
  37.6 1.5 %shard_map.94 = bf16[4,80,256]{2,1,0:T(8,128)(2,1)S(1)} custom-call(s32[48]{0:T(128)S(1)} %copy-done.4, s32[48]{0:T(128)S(1)} %copy-done.5, bf16[48,128,128]{2,1,0:T(8,128)(2,1)S(1)} %copy-done, bf16[96,16,256]{2,1,0:T(8,128)(2,1)S(1)} %bitcast.7, bf16[16,256]{1,0:T(8,128)(2,1)S(1)} %copy-done.1, bf16[32,256]{1,0:T(8,128)(2,1)S(1)} %bitcast.8), custom_call_target="tpu_custom_call" | custom-call | tf_op jit(solution)/shard_map/pallas_call | solution.py:143
  39.1 23.9 %all_to_all.27 = bf16[4,80,256]{2,1,0:T(8,128)(2,1)S(1)} all-to-all(bf16[4,80,256]{2,1,0:T(8,128)(2,1)S(1)} %shard_map.94), channel_id=1, replica_groups=mesh['x'=4,'y'=8,'z'=3,'zh'=4,'core'=2] {'zh'}, dimensions={0} | all-to-all | bytes 327680 | tf_op jit(solution)/shard_map/all_to_all | solution.py:182
  63.0 6.6 %all_gather.3.group_ref = bf16[8,80,256]{2,1,0:T(8,128)(2,1)S(1)} all-gather(bf16[4,80,256]{2,1,0:T(8,128)(2,1)S(1)} %all_to_all.27), channel_id=1, replica_groups=mesh['x'=4,'y'=8,'z'=3,'zh'=4,'core'=2] {'core'}, dimensions={0}, use_global_device_ids=true | all-gather | bytes 491520 | tf_op jit(solution)/shard_map/all_gather | solution.py:182
  69.7 0.0 copy-done.3
  69.7 2.2 %shard_map.95 = (bf16[32,256]{1,0:T(8,128)(2,1)}, bf16[12,288,128]{2,1,0:T(8,128)(2,1)S(1)}) custom-call(s32[48]{0:T(128)S(1)} %copy-done.4, s32[48]{0:T(128)S(1)} %copy-done.5, bf16[48,128,128]{2,1,0:T(8,128)(2,1)S(1)} %copy-done, bf16[8,80,256]{2,1,0:T(8,128)(2,1)S(1)} %all_gather.3.group_ref, bf16[16,256]{1,0:T(8,128)(2,1)S(1)} %copy-done.1, ...), custom_call_target="tpu_custom_call" | custom-call | tf_op jit(solution)/shard_map/pallas_call | solution.py:143
  71.9 20.1 %all_to_all.28.got_ref = bf16[12,288,128]{2,1,0:T(8,128)(2,1)S(1)} all-to-all(bf16[12,288,128]{2,1,0:T(8,128)(2,1)S(1)} %get-tuple-element.8), channel_id=1, replica_groups=mesh['x'=4,'y'=8,'z'=3,'zh'=4,'core'=2] {'x','z'}, dimensions={0} | all-to-all | bytes 1769472 | tf_op jit(solution)/shard_map/all_to_all | solution.py:203
  92.1 0.1 shard_map.96
  92.2 10.3 %all_to_all.29.got_ref = bf16[8,64,128]{2,1,0:T(8,128)(2,1)S(1)} all-to-all(bf16[8,64,128]{2,1,0:T(8,128)(2,1)S(1)} %shard_map.96), channel_id=1, replica_groups=mesh['x'=4,'y'=8,'z'=3,'zh'=4,'core'=2] {'y'}, dimensions={0} | all-to-all | bytes 262144 | tf_op jit(solution)/shard_map/all_to_all | solution.py:210
  102.5 0.6 shard_map.97
  (1 shorter events, 0.0 us)
Async XLA Ops:
  0.6 36.9 %copy-start = (bf16[48,128,128]{2,1,0:T(8,128)(2,1)S(1)}, bf16[48,128,128]{2,1,0:T(8,128)(2,1)}, u32[]{:S(2)}) copy-start(bf16[48,128,128]{2,1,0:T(8,128)(2,1)} %tiles_ref.3) | copy-start | bytes 4718596
  0.6 36.9 %copy-start.5 = (s32[48]{0:T(128)S(1)}, s32[48]{0:T(128)}, u32[]{:S(2)}) copy-start(s32[48]{0:T(128)} %cols_ref.3) | copy-start | bytes 580
  0.7 36.9 %copy-start.4 = (s32[48]{0:T(128)S(1)}, s32[48]{0:T(128)}, u32[]{:S(2)}) copy-start(s32[48]{0:T(128)} %rows_ref.3) | copy-start | bytes 580
  0.7 36.9 %copy-start.1 = (bf16[16,256]{1,0:T(8,128)(2,1)S(1)}, bf16[16,256]{1,0:T(8,128)(2,1)}, u32[]{:S(2)}) copy-start(bf16[16,256]{1,0:T(8,128)(2,1)} %weight_ref.3) | copy-start | bytes 24580
  0.7 36.9 %copy-start.2 = (bf16[256,32]{0,1:T(8,128)(2,1)S(1)}, bf16[256,32]{0,1:T(8,128)(2,1)}, u32[]{:S(2)}) copy-start(bf16[256,32]{0,1:T(8,128)(2,1)} %param.13) | copy-start | bytes 49156
  37.6 32.1 %copy-start.3 = (f32[256]{0:T(256)S(1)}, f32[256]{0:T(256)}, u32[]{:S(2)}) copy-start(f32[256]{0:T(256)} %param.9) | copy-start | bytes 3076

commit v5 on v4

--- a/solution.py
+++ b/solution.py
@@ -43,34 +43,41 @@
         for i in range(row_tiles):
             totals[i] = totals[i] + jnp.where(rows_ref[t] == i, term, 0.0)
     for i in range(row_tiles):
-        head, rest = halves(totals[i])
-        cut = slice(i * LANES, (i + 1) * LANES)
+        value = totals[i].astype(BF16)
         for n in range(out_ref.shape[0]):
-            out_ref[n, 0:part, cut] = head
-            out_ref[n, part : 2 * part, cut] = rest
+            out_ref[n, 0:part, i * LANES : (i + 1) * LANES] = value
     for n in range(out_ref.shape[0]):
-        out_ref[n, 2 * part : 3 * part] = weight_ref[...]
-        out_ref[n, 3 * part :] = cot_ref[...]
+        out_ref[n, part : 2 * part] = weight_ref[...]
+        out_ref[n, 2 * part :] = cot_ref[...]
 
 
 def middle_kernel(
-    rows_ref, cols_ref, tiles_ref, group_ref, weight_ref, norm_ref, act_ref, out_ref, pre_ref, total_ref
+    rows_ref, cols_ref, tiles_ref, held_ref, came_ref, weight_ref, norm_ref, act_ref, out_ref, pre_ref, total_ref
 ):
     my_zh, my_core = lax.axis_index("zh"), lax.axis_index("core")
     n_zh, n_core = lax.axis_size("zh"), lax.axis_size("core")
-    me, my_place = my_zh * n_core + my_core, my_core * n_zh + my_zh
+    me = my_zh * n_core + my_core
     part = weight_ref.shape[0]
     hid_part = act_ref.shape[0]
-    n_feat = group_ref.shape[0]
-    group = group_ref[...]
-    head = group[:, 0:part].reshape(n_feat * part, -1)
-    rest = group[:, part : 2 * part].reshape(n_feat * part, -1)
-    weight_all = group[:, 2 * part : 3 * part].reshape(n_feat * part, -1)
+    held, came = held_ref[...], came_ref[...]
+
+    def both(cut):
+        return jnp.concatenate([g[zh, cut] for g in (held, came) for zh in range(n_zh)], axis=0)
+
+    mixed = both(slice(0, part))
+    weight_all = both(slice(part, 2 * part))
+    low = my_core == 0
     cot = jnp.concatenate(
-        [group[core * n_zh + zh, 3 * part :] for zh in range(n_zh) for core in range(n_core)], axis=0
+        [
+            value
+            for zh in range(n_zh)
+            for h, c in [(held[zh, 2 * part :], came[zh, 2 * part :])]
+            for value in (jnp.where(low, h, c), jnp.where(low, c, h))
+        ],
+        axis=0,
     )
     norm = norm_ref[...]
-    pre = (dot(weight_all, head, TN) + dot(weight_all, rest, TN)) * norm
+    pre = dot(weight_all, mixed, TN) * norm
     pre_ref[...] = pre
     sigma = 1.0 / (1.0 + jnp.exp(-pre))
     slope = sigma * (1.0 + pre * (1.0 - sigma))
@@ -94,9 +101,7 @@
         owner, within = spot_of(cols_ref[t], row_tiles)
         total_ref[owner * row_tiles + within] += both[:part] + both[part:]
 
-    own_head = group_ref[pl.ds(my_place, 1), 0:part][0]
-    own_rest = group_ref[pl.ds(my_place, 1), part : 2 * part][0]
-    weight_part = dot(own_head, back_in, NT) + dot(own_rest, back_in, NT)
+    weight_part = dot(held_ref[pl.ds(my_zh, 1), 0:part][0], back_in, NT)
     n_first, n_rows, _ = out_ref.shape
     cols = total_ref.shape[0] // n_first
     total = total_ref[...].astype(BF16).reshape(n_first, cols * part, LANES)
@@ -170,7 +175,7 @@
     )
     group = call(
         forward_kernel,
-        shape((lax.axis_size("zh"), 3 * part + hid_part, rows_dev), BF16),
+        shape((lax.axis_size("zh"), 2 * part + hid_part, rows_dev), BF16),
         [SMEM, SMEM, VMEM, VMEM, VMEM, VMEM],
         tile_rows,
         tile_cols,
@@ -179,7 +184,8 @@
         weight,
         cotangent.T,
     )
-    group = lax.all_gather(lax.all_to_all(group, "zh", 0, 0), "core", axis=0, tiled=True)
+    held = lax.all_to_all(group, "zh", 0, 0)
+    came = lax.ppermute(held, "core", [(0, 1), (1, 0)])
     own = row_tiles * part
     weight_rows = part * hidden // tile_len
     activated, sent = call(
@@ -188,11 +194,12 @@
             shape((hid_part, rows_dev), BF16),
             shape((n_first, n_second * own + weight_rows, tile_len), BF16),
         ),
-        [SMEM, SMEM, VMEM, VMEM, VMEM, VMEM],
+        [SMEM, SMEM, VMEM, VMEM, VMEM, VMEM, VMEM],
         tile_rows,
         tile_cols,
         tile_vals,
-        group,
+        held,
+        came,
         weight,
         norm,
         scratch=(

time: 104 us -> 105 us (level)
  blocking collectives: 97.1 us -> 90.2 us
  starting transfers between devices: 0 us -> 6.87 us
    ppermute x0 -> x1, starting transfers between devices: none -> 6.87 us  [per_device(): came = lax.ppermute(held, 'core', [(0, 1), (1, 0)])]
    all_gather x1 -> x0, blocking collectives: 6.65 us -> none  [per_device(): lax.all_gather(lax.all_to_all(group, 'zh', 0, 0), 'core', axis=0, tiled=T...]
  transfers between devices with their start and end apart: 0 -> 1, of which waited for: 0 -> 1; matrix products, arithmetic and copies ran while one was open for 0% -> 0% of each run, Pallas kernels for 0% -> 0%
where the time goes in v5:
time: 105 us; the launch traced here: 104 us
  blocking collectives  90.2 us (86%)
  starting transfers between devices  6.87 us (7%)
  Pallas kernels  4.43 us (4%)
    all_to_all x1, blocking collectives, per_device(): held = lax.all_to_all(group, 'zh', 0, 0)  23.8 us
    all_to_all x1, blocking collectives, per_device(): lax.all_to_all(jnp.broadcast_to(block[None], (n_first,) + block.shape), F...  21.3 us
    all_to_all x1, blocking collectives, per_device(): got = lax.all_to_all(sent, FIRST, 0, 0)  20.1 us
    all_to_all x1, blocking collectives, per_device(): block = lax.all_to_all(block, SECOND, 0, 0)  14.7 us
    all_to_all x1, blocking collectives, per_device(): got = lax.all_to_all(sent, SECOND, 0, 0)  10.3 us
    ppermute x1, starting transfers between devices, per_device(): came = lax.ppermute(held, 'core', [(0, 1), (1, 0)])  6.87 us
    pallas_call x4, Pallas kernels, call(): pl.pallas_call(kernel, out_shape=outs, in_specs=in_specs, out_specs=jax.t...  4.43 us
  transfers between devices with their start and end apart: 1, of which 1 were waited for; matrix products, arithmetic and copies ran while one was open for 0% of the time, Pallas kernels for 0%

profile of v5, /device:TPU:1, one launch (start us, length us, event | category | flops | bytes accessed | tf_op | source)
XLA Modules:
  0.0 104.0 jit_solution(15637211954391958535)
XLA Ops:
  0.6 0.0 copy-start
  0.6 0.0 copy-start.5
  0.7 0.0 copy-start.4
  0.7 0.0 copy-start.1
  0.7 0.0 copy-start.2
  0.7 0.8 fusion
  1.5 14.7 %all_to_all.25 = bf16[8,16,256]{2,1,0:T(8,128)(2,1)S(1)} all-to-all(bf16[8,16,256]{2,1,0:T(8,128)(2,1)S(1)} %broadcast_in_dim.6), channel_id=1, replica_groups=mesh['x'=4,'y'=8,'z'=3,'zh'=4,'core'=2] {'y'}, dimensions={0} | all-to-all | bytes 131072 | tf_op jit(solution)/shard_map/all_to_all | solution.py:172
  16.2 0.1 broadcast_in_dim.7
  16.3 21.3 %all_to_all.26 = bf16[12,8,16,256]{3,2,1,0:T(8,128)(2,1)S(1)} all-to-all(bf16[12,8,16,256]{3,2,1,0:T(8,128)(2,1)S(1)} %broadcast_in_dim.7), channel_id=1, replica_groups=mesh['x'=4,'y'=8,'z'=3,'zh'=4,'core'=2] {'x','z'}, dimensions={0} | all-to-all | bytes 1572864 | tf_op jit(solution)/shard_map/all_to_all | solution.py:173
  37.5 0.0 copy-start.3
  37.5 0.0 copy-done
  37.6 0.0 copy-done.5
  37.6 0.0 copy-done.4
  37.6 0.0 copy-done.1
  37.6 0.0 copy-done.2
  37.6 1.5 %shard_map.94 = bf16[4,64,256]{2,1,0:T(8,128)(2,1)S(1)} custom-call(s32[48]{0:T(128)S(1)} %copy-done.4, s32[48]{0:T(128)S(1)} %copy-done.5, bf16[48,128,128]{2,1,0:T(8,128)(2,1)S(1)} %copy-done, bf16[96,16,256]{2,1,0:T(8,128)(2,1)S(1)} %bitcast.7, bf16[16,256]{1,0:T(8,128)(2,1)S(1)} %copy-done.1, bf16[32,256]{1,0:T(8,128)(2,1)S(1)} %bitcast.8), custom_call_target="tpu_custom_call" | custom-call | tf_op jit(solution)/shard_map/pallas_call | solution.py:148
  39.1 23.8 %all_to_all.27.held_ref = bf16[4,64,256]{2,1,0:T(8,128)(2,1)S(1)} all-to-all(bf16[4,64,256]{2,1,0:T(8,128)(2,1)S(1)} %shard_map.94), channel_id=1, replica_groups=mesh['x'=4,'y'=8,'z'=3,'zh'=4,'core'=2] {'zh'}, dimensions={0} | all-to-all | bytes 262144 | tf_op jit(solution)/shard_map/all_to_all | solution.py:187
  62.8 6.9 %collective-permute-start = (bf16[4,64,256]{2,1,0:T(8,128)(2,1)S(1)}, bf16[4,64,256]{2,1,0:T(8,128)(2,1)S(1)}, u32[]{:S(2)}, u32[]{:S(2)}) collective-permute-start(bf16[4,64,256]{2,1,0:T(8,128)(2,1)S(1)} %all_to_all.27.held_ref), channel_id=1, source_target_pairs={{0,1},{1,0},{2,3},{3,2},{4,5},{5,4},{6,7},{7,6},{8,9},{9,8},{10,11... | collective-permute-start | bytes 393224 | tf_op jit(solution)/shard_map/ppermute | solution.py:188
  69.7 1.0 collective-permute-done.came_ref
  70.7 0.0 copy-done.3
  70.7 2.2 %shard_map.95 = (bf16[32,256]{1,0:T(8,128)(2,1)}, bf16[12,288,128]{2,1,0:T(8,128)(2,1)S(1)}) custom-call(s32[48]{0:T(128)S(1)} %copy-done.4, s32[48]{0:T(128)S(1)} %copy-done.5, bf16[48,128,128]{2,1,0:T(8,128)(2,1)S(1)} %copy-done, bf16[4,64,256]{2,1,0:T(8,128)(2,1)S(1)} %all_to_all.27.held_ref, bf16[4,64,256]{2,1,0:T(8,128)(2,1)S(1)} %collective-permute-done.came_ref, ...), custom_call_target="tpu_custom_call" | custom-call | tf_op jit(solution)/shard_map/pallas_call | solution.py:148
  72.9 20.1 %all_to_all.28.got_ref = bf16[12,288,128]{2,1,0:T(8,128)(2,1)S(1)} all-to-all(bf16[12,288,128]{2,1,0:T(8,128)(2,1)S(1)} %get-tuple-element.8), channel_id=1, replica_groups=mesh['x'=4,'y'=8,'z'=3,'zh'=4,'core'=2] {'x','z'}, dimensions={0} | all-to-all | bytes 1769472 | tf_op jit(solution)/shard_map/all_to_all | solution.py:210
  93.0 0.1 shard_map.96
  93.1 10.3 %all_to_all.29.got_ref = bf16[8,64,128]{2,1,0:T(8,128)(2,1)S(1)} all-to-all(bf16[8,64,128]{2,1,0:T(8,128)(2,1)S(1)} %shard_map.96), channel_id=1, replica_groups=mesh['x'=4,'y'=8,'z'=3,'zh'=4,'core'=2] {'y'}, dimensions={0} | all-to-all | bytes 262144 | tf_op jit(solution)/shard_map/all_to_all | solution.py:217
  103.4 0.6 shard_map.97
  (1 shorter events, 0.0 us)
Async XLA Ops:
  0.6 36.9 %copy-start = (bf16[48,128,128]{2,1,0:T(8,128)(2,1)S(1)}, bf16[48,128,128]{2,1,0:T(8,128)(2,1)}, u32[]{:S(2)}) copy-start(bf16[48,128,128]{2,1,0:T(8,128)(2,1)} %tiles_ref.3) | copy-start | bytes 4718596
  0.6 36.9 %copy-start.5 = (s32[48]{0:T(128)S(1)}, s32[48]{0:T(128)}, u32[]{:S(2)}) copy-start(s32[48]{0:T(128)} %cols_ref.3) | copy-start | bytes 580
  0.7 36.9 %copy-start.4 = (s32[48]{0:T(128)S(1)}, s32[48]{0:T(128)}, u32[]{:S(2)}) copy-start(s32[48]{0:T(128)} %rows_ref.3) | copy-start | bytes 580
  0.7 36.9 %copy-start.1 = (bf16[16,256]{1,0:T(8,128)(2,1)S(1)}, bf16[16,256]{1,0:T(8,128)(2,1)}, u32[]{:S(2)}) copy-start(bf16[16,256]{1,0:T(8,128)(2,1)} %weight_ref.3) | copy-start | bytes 24580
  0.7 36.9 %copy-start.2 = (bf16[256,32]{0,1:T(8,128)(2,1)S(1)}, bf16[256,32]{0,1:T(8,128)(2,1)}, u32[]{:S(2)}) copy-start(bf16[256,32]{0,1:T(8,128)(2,1)} %param.13) | copy-start | bytes 49156
  37.5 33.1 %copy-start.3 = (f32[256]{0:T(256)S(1)}, f32[256]{0:T(256)}, u32[]{:S(2)}) copy-start(f32[256]{0:T(256)} %param.9) | copy-start | bytes 3076
  62.8 7.8 %collective-permute-start = (bf16[4,64,256]{2,1,0:T(8,128)(2,1)S(1)}, bf16[4,64,256]{2,1,0:T(8,128)(2,1)S(1)}, u32[]{:S(2)}, u32[]{:S(2)}) collective-permute-start(bf16[4,64,256]{2,1,0:T(8,128)(2,1)S(1)} %all_to_all.27.held_ref), channel_id=1, source_target_pairs={{0,1},{1,0},{2,3},{3,2},{4,5},{5,4},{6,7},{7,6},{8,9},{9,8},{10,11... | collective-permute-start | bytes 393224 | tf_op jit(solution)/shard_map/ppermute | solution.py:188

commit v6 on v4

--- a/solution.py
+++ b/solution.py
@@ -37,7 +37,7 @@
     row_tiles = cot_ref.shape[1] // LANES
     totals = [jnp.zeros((part, LANES), F32) for _ in range(row_tiles)]
     for t in range(tiles_ref.shape[0]):
-        owner, within = spot_of(cols_ref[t], row_tiles)
+        owner, within = lax.div(cols_ref[t], row_tiles), lax.rem(cols_ref[t], row_tiles)
         nodes = nodes_ref[owner, :, pl.ds(pl.multiple_of(within * LANES, LANES), LANES)]
         term = dot(nodes, tiles_ref[t], NT)
         for i in range(row_tiles):
@@ -163,11 +163,9 @@
     shape = jax.ShapeDtypeStruct
 
     block = (features.T.astype(F32) * norm_scale[None, :]).astype(BF16)
-    block = jnp.broadcast_to(block[None], (n_second,) + block.shape)
-    block = lax.all_to_all(block, SECOND, 0, 0)
-    block = lax.all_to_all(
-        jnp.broadcast_to(block[None], (n_first,) + block.shape), FIRST, 0, 0
-    )
+    for axes in OUT:
+        block = jnp.broadcast_to(block[None], (lax.axis_size(axes),) + block.shape)
+        block = lax.all_to_all(block, axes, 0, 0)
     group = call(
         forward_kernel,
         shape((lax.axis_size("zh"), 3 * part + hid_part, rows_dev), BF16),
@@ -218,6 +216,7 @@
     return (activated.T, weight_grad, feature_grad.T)
 
 
+OUT = (("y", "z"), "x")
 FIRST, SECOND = ("x", "z"), "y"
 
 

time: 104 us -> 103 us (level)
    all_to_all x2, blocking collectives: 36 us -> 34.9 us  [per_device(): block = lax.all_to_all(block, axes, 0, 0)]
where the time goes in v6:
time: 103 us; the launch traced here: 102 us
  blocking collectives  96.3 us (93%)
  Pallas kernels  4.49 us (4%)
    all_to_all x2, blocking collectives, per_device(): block = lax.all_to_all(block, axes, 0, 0)  34.9 us
    all_to_all x1, blocking collectives, per_device(): lax.all_to_all(group, 'zh', 0, 0)  23.8 us
    all_to_all x1, blocking collectives, per_device(): got = lax.all_to_all(sent, FIRST, 0, 0)  20.1 us
    all_to_all x1, blocking collectives, per_device(): got = lax.all_to_all(sent, SECOND, 0, 0)  11.3 us
    all_gather x1, blocking collectives, per_device(): lax.all_gather(lax.all_to_all(group, 'zh', 0, 0), 'core', axis=0, tiled=T...  6.26 us
    pallas_call x4, Pallas kernels, call(): pl.pallas_call(kernel, out_shape=outs, in_specs=in_specs, out_specs=jax.t...  4.49 us

profile of v6, /device:TPU:1, one launch (start us, length us, event | category | flops | bytes accessed | tf_op | source)
XLA Modules:
  0.0 102.4 jit_solution(14150207870413556720)
XLA Ops:
  0.6 0.7 fusion
  1.3 0.0 copy-start
  1.3 0.0 copy-start.1
  1.3 0.0 copy-start.2
  1.4 0.0 copy-start.4
  1.4 0.0 copy-start.5
  1.4 21.1 %all_to_all.25 = bf16[24,16,256]{2,1,0:T(8,128)(2,1)S(1)} all-to-all(bf16[24,16,256]{2,1,0:T(8,128)(2,1)S(1)} %broadcast_in_dim.6), channel_id=1, replica_groups=mesh['x'=4,'y'=8,'z'=3,'zh'=4,'core'=2] {'y','z'}, dimensions={0} | all-to-all | bytes 393216 | tf_op jit(solution)/shard_map/all_to_all | solution.py:168
  22.5 0.1 broadcast_in_dim.7
  22.6 13.7 %all_to_all.26 = bf16[4,24,16,256]{3,2,1,0:T(8,128)(2,1)S(1)} all-to-all(bf16[4,24,16,256]{3,2,1,0:T(8,128)(2,1)S(1)} %broadcast_in_dim.7), channel_id=1, replica_groups=mesh['x'=4,'y'=8,'z'=3,'zh'=4,'core'=2] {'x'}, dimensions={0} | all-to-all | bytes 1572864 | tf_op jit(solution)/shard_map/all_to_all | solution.py:168
  36.3 0.0 copy-done
  36.3 0.0 copy-done.1
  36.3 0.0 copy-done.2
  36.4 0.0 copy-done.4
  36.4 0.0 copy-done.5
  36.4 0.0 copy-start.3
  36.4 1.5 %shard_map.94 = bf16[4,80,256]{2,1,0:T(8,128)(2,1)S(1)} custom-call(s32[48]{0:T(128)S(1)} %copy-done.4, s32[48]{0:T(128)S(1)} %copy-done.5, bf16[48,128,128]{2,1,0:T(8,128)(2,1)S(1)} %copy-done, bf16[96,16,256]{2,1,0:T(8,128)(2,1)S(1)} %bitcast.7, bf16[16,256]{1,0:T(8,128)(2,1)S(1)} %copy-done.1, bf16[32,256]{1,0:T(8,128)(2,1)S(1)} %bitcast.8), custom_call_target="tpu_custom_call" | custom-call | tf_op jit(solution)/shard_map/pallas_call | solution.py:143
  37.9 23.8 %all_to_all.27 = bf16[4,80,256]{2,1,0:T(8,128)(2,1)S(1)} all-to-all(bf16[4,80,256]{2,1,0:T(8,128)(2,1)S(1)} %shard_map.94), channel_id=1, replica_groups=mesh['x'=4,'y'=8,'z'=3,'zh'=4,'core'=2] {'zh'}, dimensions={0} | all-to-all | bytes 327680 | tf_op jit(solution)/shard_map/all_to_all | solution.py:180
  61.7 6.3 %all_gather.3.group_ref = bf16[8,80,256]{2,1,0:T(8,128)(2,1)S(1)} all-gather(bf16[4,80,256]{2,1,0:T(8,128)(2,1)S(1)} %all_to_all.27), channel_id=1, replica_groups=mesh['x'=4,'y'=8,'z'=3,'zh'=4,'core'=2] {'core'}, dimensions={0}, use_global_device_ids=true | all-gather | bytes 491520 | tf_op jit(solution)/shard_map/all_gather | solution.py:180
  68.0 0.0 copy-done.3
  68.0 2.3 %shard_map.95 = (bf16[32,256]{1,0:T(8,128)(2,1)}, bf16[12,288,128]{2,1,0:T(8,128)(2,1)S(1)}) custom-call(s32[48]{0:T(128)S(1)} %copy-done.4, s32[48]{0:T(128)S(1)} %copy-done.5, bf16[48,128,128]{2,1,0:T(8,128)(2,1)S(1)} %copy-done, bf16[8,80,256]{2,1,0:T(8,128)(2,1)S(1)} %all_gather.3.group_ref, bf16[16,256]{1,0:T(8,128)(2,1)S(1)} %copy-done.1, ...), custom_call_target="tpu_custom_call" | custom-call | tf_op jit(solution)/shard_map/pallas_call | solution.py:143
  70.2 20.1 %all_to_all.28.got_ref = bf16[12,288,128]{2,1,0:T(8,128)(2,1)S(1)} all-to-all(bf16[12,288,128]{2,1,0:T(8,128)(2,1)S(1)} %get-tuple-element.8), channel_id=1, replica_groups=mesh['x'=4,'y'=8,'z'=3,'zh'=4,'core'=2] {'x','z'}, dimensions={0} | all-to-all | bytes 1769472 | tf_op jit(solution)/shard_map/all_to_all | solution.py:201
  90.3 0.1 shard_map.96
  90.4 11.3 %all_to_all.29.got_ref = bf16[8,64,128]{2,1,0:T(8,128)(2,1)S(1)} all-to-all(bf16[8,64,128]{2,1,0:T(8,128)(2,1)S(1)} %shard_map.96), channel_id=1, replica_groups=mesh['x'=4,'y'=8,'z'=3,'zh'=4,'core'=2] {'y'}, dimensions={0} | all-to-all | bytes 262144 | tf_op jit(solution)/shard_map/all_to_all | solution.py:208
  101.7 0.6 shard_map.97
  (1 shorter events, 0.0 us)
Async XLA Ops:
  1.3 35.0 %copy-start = (bf16[48,128,128]{2,1,0:T(8,128)(2,1)S(1)}, bf16[48,128,128]{2,1,0:T(8,128)(2,1)}, u32[]{:S(2)}) copy-start(bf16[48,128,128]{2,1,0:T(8,128)(2,1)} %tiles_ref.3) | copy-start | bytes 4718596
  1.3 35.0 %copy-start.1 = (bf16[16,256]{1,0:T(8,128)(2,1)S(1)}, bf16[16,256]{1,0:T(8,128)(2,1)}, u32[]{:S(2)}) copy-start(bf16[16,256]{1,0:T(8,128)(2,1)} %weight_ref.3) | copy-start | bytes 24580
  1.3 35.0 %copy-start.2 = (bf16[256,32]{0,1:T(8,128)(2,1)S(1)}, bf16[256,32]{0,1:T(8,128)(2,1)}, u32[]{:S(2)}) copy-start(bf16[256,32]{0,1:T(8,128)(2,1)} %param.13) | copy-start | bytes 49156
  1.4 35.0 %copy-start.4 = (s32[48]{0:T(128)S(1)}, s32[48]{0:T(128)}, u32[]{:S(2)}) copy-start(s32[48]{0:T(128)} %rows_ref.3) | copy-start | bytes 580
  1.4 35.0 %copy-start.5 = (s32[48]{0:T(128)S(1)}, s32[48]{0:T(128)}, u32[]{:S(2)}) copy-start(s32[48]{0:T(128)} %cols_ref.3) | copy-start | bytes 580
  36.4 31.6 %copy-start.3 = (f32[256]{0:T(256)S(1)}, f32[256]{0:T(256)}, u32[]{:S(2)}) copy-start(f32[256]{0:T(256)} %param.9) | copy-start | bytes 3076

commit v7 on v6

--- a/solution.py
+++ b/solution.py
@@ -35,13 +35,19 @@
 def forward_kernel(rows_ref, cols_ref, tiles_ref, nodes_ref, weight_ref, cot_ref, out_ref):
     part = weight_ref.shape[0]
     row_tiles = cot_ref.shape[1] // LANES
-    totals = [jnp.zeros((part, LANES), F32) for _ in range(row_tiles)]
-    for t in range(tiles_ref.shape[0]):
-        owner, within = lax.div(cols_ref[t], row_tiles), lax.rem(cols_ref[t], row_tiles)
-        nodes = nodes_ref[owner, :, pl.ds(pl.multiple_of(within * LANES, LANES), LANES)]
-        term = dot(nodes, tiles_ref[t], NT)
-        for i in range(row_tiles):
-            totals[i] = totals[i] + jnp.where(rows_ref[t] == i, term, 0.0)
+    sums = jnp.zeros((row_tiles * part, LANES), F32)
+    for t in range(0, tiles_ref.shape[0], 2):
+        lefts = []
+        for u in (t, t + 1):
+            owner, within = lax.div(cols_ref[u], row_tiles), lax.rem(cols_ref[u], row_tiles)
+            nodes = nodes_ref[owner, :, pl.ds(pl.multiple_of(within * LANES, LANES), LANES)]
+            none = jnp.zeros_like(nodes)
+            lefts.append(
+                jnp.concatenate([jnp.where(rows_ref[u] == i, nodes, none) for i in range(row_tiles)], axis=0)
+            )
+        right = jnp.concatenate([tiles_ref[t], tiles_ref[t + 1]], axis=1)
+        sums = sums + dot(jnp.concatenate(lefts, axis=1), right, NT)
+    totals = [sums[i * part : (i + 1) * part] for i in range(row_tiles)]
     for i in range(row_tiles):
         head, rest = halves(totals[i])
         cut = slice(i * LANES, (i + 1) * LANES)
@@ -119,7 +125,8 @@
         out_ref[n, own:] = total[n_peer * own :].astype(BF16)
 
 
-def end_kernel(got_ref, norm_ref, grad_ref, weight_ref):
+def end_kernel(got_ref, norm_ref, act_ref, grad_ref, weight_ref, out_act_ref):
+    out_act_ref[...] = act_ref[...]
     total = got_ref[0].astype(F32)
     for n in range(1, got_ref.shape[0]):
         total = total + got_ref[n].astype(F32)
@@ -206,12 +213,17 @@
         got,
     )
     got = lax.all_to_all(sent, SECOND, 0, 0)
-    feature_grad, weight_grad = call(
+    feature_grad, weight_grad, activated = call(
         end_kernel,
-        (shape((part, rows_dev), BF16), shape((part, hidden), F32)),
-        [VMEM, VMEM],
+        (
+            shape((part, rows_dev), BF16),
+            shape((part, hidden), F32),
+            shape((hid_part, rows_dev), BF16),
+        ),
+        [VMEM, VMEM, VMEM],
         got,
         norm,
+        activated,
     )
     return (activated.T, weight_grad, feature_grad.T)
 

time: 103 us -> 103 us (level)
  no operation moved by 1% of the time
where the time goes in v7:
time: 103 us; the launch traced here: 102 us
  blocking collectives  96.4 us (94%)
  Pallas kernels  3.74 us (4%)
    all_to_all x2, blocking collectives, per_device(): block = lax.all_to_all(block, axes, 0, 0)  34.9 us
    all_to_all x1, blocking collectives, per_device(): lax.all_to_all(group, 'zh', 0, 0)  23.8 us
    all_to_all x1, blocking collectives, per_device(): got = lax.all_to_all(sent, FIRST, 0, 0)  20.1 us
    all_to_all x1, blocking collectives, per_device(): got = lax.all_to_all(sent, SECOND, 0, 0)  11.3 us
    all_gather x1, blocking collectives, per_device(): lax.all_gather(lax.all_to_all(group, 'zh', 0, 0), 'core', axis=0, tiled=T...  6.26 us
    pallas_call x4, Pallas kernels, call(): pl.pallas_call(kernel, out_shape=outs, in_specs=in_specs, out_specs=jax.t...  3.74 us

profile of v7, /device:TPU:1, one launch (start us, length us, event | category | flops | bytes accessed | tf_op | source)
XLA Modules:
  0.0 101.6 jit_solution(15354156452783417508)
XLA Ops:
  0.6 0.7 fusion
  1.3 0.0 copy-start
  1.3 0.0 copy-start.1
  1.3 0.0 copy-start.2
  1.4 0.0 copy-start.4
  1.4 0.0 copy-start.5
  1.4 21.1 %all_to_all.25 = bf16[24,16,256]{2,1,0:T(8,128)(2,1)S(1)} all-to-all(bf16[24,16,256]{2,1,0:T(8,128)(2,1)S(1)} %broadcast_in_dim.6), channel_id=1, replica_groups=mesh['x'=4,'y'=8,'z'=3,'zh'=4,'core'=2] {'y','z'}, dimensions={0} | all-to-all | bytes 393216 | tf_op jit(solution)/shard_map/all_to_all | solution.py:175
  22.5 0.1 broadcast_in_dim.7
  22.6 13.7 %all_to_all.26 = bf16[4,24,16,256]{3,2,1,0:T(8,128)(2,1)S(1)} all-to-all(bf16[4,24,16,256]{3,2,1,0:T(8,128)(2,1)S(1)} %broadcast_in_dim.7), channel_id=1, replica_groups=mesh['x'=4,'y'=8,'z'=3,'zh'=4,'core'=2] {'x'}, dimensions={0} | all-to-all | bytes 1572864 | tf_op jit(solution)/shard_map/all_to_all | solution.py:175
  36.3 0.0 copy-done
  36.3 0.0 copy-done.1
  36.3 0.0 copy-done.2
  36.4 0.0 copy-done.4
  36.4 0.0 copy-done.5
  36.4 0.0 copy-start.3
  36.4 1.2 %shard_map.94 = bf16[4,80,256]{2,1,0:T(8,128)(2,1)S(1)} custom-call(s32[48]{0:T(128)S(1)} %copy-done.4, s32[48]{0:T(128)S(1)} %copy-done.5, bf16[48,128,128]{2,1,0:T(8,128)(2,1)S(1)} %copy-done, bf16[96,16,256]{2,1,0:T(8,128)(2,1)S(1)} %bitcast.7, bf16[16,256]{1,0:T(8,128)(2,1)S(1)} %copy-done.1, bf16[32,256]{1,0:T(8,128)(2,1)S(1)} %bitcast.8), custom_call_target="tpu_custom_call" | custom-call | tf_op jit(solution)/shard_map/pallas_call | solution.py:150
  37.6 23.8 %all_to_all.27 = bf16[4,80,256]{2,1,0:T(8,128)(2,1)S(1)} all-to-all(bf16[4,80,256]{2,1,0:T(8,128)(2,1)S(1)} %shard_map.94), channel_id=1, replica_groups=mesh['x'=4,'y'=8,'z'=3,'zh'=4,'core'=2] {'zh'}, dimensions={0} | all-to-all | bytes 327680 | tf_op jit(solution)/shard_map/all_to_all | solution.py:187
  61.4 6.3 %all_gather.3.group_ref = bf16[8,80,256]{2,1,0:T(8,128)(2,1)S(1)} all-gather(bf16[4,80,256]{2,1,0:T(8,128)(2,1)S(1)} %all_to_all.27), channel_id=1, replica_groups=mesh['x'=4,'y'=8,'z'=3,'zh'=4,'core'=2] {'core'}, dimensions={0}, use_global_device_ids=true | all-gather | bytes 491520 | tf_op jit(solution)/shard_map/all_gather | solution.py:187
  67.7 0.0 copy-done.3
  67.7 1.8 %shard_map.95 = (bf16[32,256]{1,0:T(8,128)(2,1)S(1)}, bf16[12,288,128]{2,1,0:T(8,128)(2,1)S(1)}) custom-call(s32[48]{0:T(128)S(1)} %copy-done.4, s32[48]{0:T(128)S(1)} %copy-done.5, bf16[48,128,128]{2,1,0:T(8,128)(2,1)S(1)} %copy-done, bf16[8,80,256]{2,1,0:T(8,128)(2,1)S(1)} %all_gather.3.group_ref, bf16[16,256]{1,0:T(8,128)(2,1)S(1)} %copy-done.1, ...), custom_call_target="tpu_custom_call" | custom-call | tf_op jit(solution)/shard_map/pallas_call | solution.py:150
  69.5 20.1 %all_to_all.28.got_ref = bf16[12,288,128]{2,1,0:T(8,128)(2,1)S(1)} all-to-all(bf16[12,288,128]{2,1,0:T(8,128)(2,1)S(1)} %get-tuple-element.8), channel_id=1, replica_groups=mesh['x'=4,'y'=8,'z'=3,'zh'=4,'core'=2] {'x','z'}, dimensions={0} | all-to-all | bytes 1769472 | tf_op jit(solution)/shard_map/all_to_all | solution.py:208
  89.6 0.1 shard_map.96
  89.7 11.3 %all_to_all.29.got_ref = bf16[8,64,128]{2,1,0:T(8,128)(2,1)S(1)} all-to-all(bf16[8,64,128]{2,1,0:T(8,128)(2,1)S(1)} %shard_map.96), channel_id=1, replica_groups=mesh['x'=4,'y'=8,'z'=3,'zh'=4,'core'=2] {'y'}, dimensions={0} | all-to-all | bytes 262144 | tf_op jit(solution)/shard_map/all_to_all | solution.py:215
  101.0 0.6 shard_map.97
  (1 shorter events, 0.0 us)
Async XLA Ops:
  1.3 35.0 %copy-start = (bf16[48,128,128]{2,1,0:T(8,128)(2,1)S(1)}, bf16[48,128,128]{2,1,0:T(8,128)(2,1)}, u32[]{:S(2)}) copy-start(bf16[48,128,128]{2,1,0:T(8,128)(2,1)} %tiles_ref.3) | copy-start | bytes 4718596
  1.3 35.0 %copy-start.1 = (bf16[16,256]{1,0:T(8,128)(2,1)S(1)}, bf16[16,256]{1,0:T(8,128)(2,1)}, u32[]{:S(2)}) copy-start(bf16[16,256]{1,0:T(8,128)(2,1)} %weight_ref.3) | copy-start | bytes 24580
  1.3 35.0 %copy-start.2 = (bf16[256,32]{0,1:T(8,128)(2,1)S(1)}, bf16[256,32]{0,1:T(8,128)(2,1)}, u32[]{:S(2)}) copy-start(bf16[256,32]{0,1:T(8,128)(2,1)} %param.13) | copy-start | bytes 49156
  1.4 35.0 %copy-start.4 = (s32[48]{0:T(128)S(1)}, s32[48]{0:T(128)}, u32[]{:S(2)}) copy-start(s32[48]{0:T(128)} %rows_ref.3) | copy-start | bytes 580
  1.4 35.0 %copy-start.5 = (s32[48]{0:T(128)S(1)}, s32[48]{0:T(128)}, u32[]{:S(2)}) copy-start(s32[48]{0:T(128)} %cols_ref.3) | copy-start | bytes 580
  36.4 31.3 %copy-start.3 = (f32[256]{0:T(256)S(1)}, f32[256]{0:T(256)}, u32[]{:S(2)}) copy-start(f32[256]{0:T(256)} %param.9) | copy-start | bytes 3076

commit v8 on v7

--- a/solution.py
+++ b/solution.py
@@ -24,12 +24,15 @@
     return lax.dot_general(left, right, dims, preferred_element_type=F32)
 
 
-def spot_of(tile, row_tiles):
-    n_z, n_y = lax.axis_size("z"), lax.axis_size("y")
+def spot_of(tile, row_tiles, orders):
     within, owner = lax.rem(tile, row_tiles), lax.div(tile, row_tiles)
-    z, owner = lax.rem(owner, n_z), lax.div(owner, n_z)
-    y, x = lax.rem(owner, n_y), lax.div(owner, n_y)
-    return (x * n_z + z) * n_y + y, within
+    where = {}
+    for axis in reversed(ROW):
+        where[axis], owner = lax.rem(owner, lax.axis_size(axis)), lax.div(owner, lax.axis_size(axis))
+    spot = 0
+    for axis in [axis for order in orders for axis in order]:
+        spot = spot * lax.axis_size(axis) + where[axis]
+    return spot, within
 
 
 def forward_kernel(rows_ref, cols_ref, tiles_ref, nodes_ref, weight_ref, cot_ref, out_ref):
@@ -39,7 +42,7 @@
     for t in range(0, tiles_ref.shape[0], 2):
         lefts = []
         for u in (t, t + 1):
-            owner, within = lax.div(cols_ref[u], row_tiles), lax.rem(cols_ref[u], row_tiles)
+            owner, within = spot_of(cols_ref[u], row_tiles, OUT[::-1])
             nodes = nodes_ref[owner, :, pl.ds(pl.multiple_of(within * LANES, LANES), LANES)]
             none = jnp.zeros_like(nodes)
             lefts.append(
@@ -97,7 +100,7 @@
         for i in range(1, row_tiles):
             left = jnp.where(rows_ref[t] == i, back_tiles[i], left)
         both = dot(left, tiles_ref[t], NN)
-        owner, within = spot_of(cols_ref[t], row_tiles)
+        owner, within = spot_of(cols_ref[t], row_tiles, BACK)
         total_ref[owner * row_tiles + within] += both[:part] + both[part:]
 
     own_head = group_ref[pl.ds(my_place, 1), 0:part][0]
@@ -163,8 +166,8 @@
     row_tiles = rows_dev // tile_len
     hid_part = cotangent.shape[1]
     hidden = weight.shape[1]
-    n_first = lax.axis_size(FIRST)
-    n_second = lax.axis_size(SECOND)
+    n_first = lax.axis_size(BACK[0])
+    n_second = lax.axis_size(BACK[1])
     col_tiles = n_first * n_second * row_tiles
     norm = norm_scale.reshape(1, rows_dev)
     shape = jax.ShapeDtypeStruct
@@ -205,14 +208,14 @@
             pltpu.VMEM((col_tiles, part, tile_len), F32),
         ),
     )
-    got = lax.all_to_all(sent, FIRST, 0, 0)
+    got = lax.all_to_all(sent, BACK[0], 0, 0)
     sent = call(
         functools.partial(relay_kernel, own=own),
         shape((n_second, own + weight_rows, tile_len), BF16),
         [VMEM],
         got,
     )
-    got = lax.all_to_all(sent, SECOND, 0, 0)
+    got = lax.all_to_all(sent, BACK[1], 0, 0)
     feature_grad, weight_grad, activated = call(
         end_kernel,
         (
@@ -228,18 +231,19 @@
     return (activated.T, weight_grad, feature_grad.T)
 
 
-OUT = (("y", "z"), "x")
-FIRST, SECOND = ("x", "z"), "y"
+ROW, FEAT = ("x", "yh", "yl", "z"), ("zh", "core")
+OUT = (("z", "yh"), ("yl", "x"))
+BACK = (("yl", "x"), ("z", "yh"))
 
 
 def axes_of(rows, feats):
-    return ((4, 8, 3) if rows == 96 else (2, rows // 4, 2)) + (feats // 2, 2)
+    return ((4, 4, 2, 3) if rows == 96 else (2, rows // 4, 2, 1)) + (feats // 2, 2)
 
 
 def solution(mesh):
     sizes = axes_of(mesh.shape["row"], mesh.shape["feat"])
-    fine = Mesh(mesh.devices.reshape(sizes), ("x", "y", "z", "zh", "core"))
-    row, feat = ("x", "y", "z"), ("zh", "core")
+    fine = Mesh(mesh.devices.reshape(sizes), ROW + FEAT)
+    row, feat = ROW, FEAT
     placed = (
         P(row, feat),
         P(feat, None),

time: 103 us -> 98.6 us (0.957)
  blocking collectives: 96.4 us -> 91.7 us
    all_to_all x2, blocking collectives: 31.4 us -> 27.2 us  [the longest x1 15.5 us: per_device(): got = lax.all_to_all(sent, BACK[0], 0, 0)]
    all_to_all x2, blocking collectives: 34.9 us -> 33.8 us  [per_device(): block = lax.all_to_all(block, axes, 0, 0)]
where the time goes in v8:
time: 98.6 us; the launch traced here: 97.6 us
  blocking collectives  91.7 us (93%)
  Pallas kernels  4.22 us (4%)
    all_to_all x2, blocking collectives, per_device(): block = lax.all_to_all(block, axes, 0, 0)  33.8 us
    all_to_all x1, blocking collectives, per_device(): lax.all_to_all(group, 'zh', 0, 0)  23.9 us
    all_to_all x1, blocking collectives, per_device(): got = lax.all_to_all(sent, BACK[0], 0, 0)  15.5 us
    all_to_all x1, blocking collectives, per_device(): got = lax.all_to_all(sent, BACK[1], 0, 0)  11.6 us
    all_gather x1, blocking collectives, per_device(): lax.all_gather(lax.all_to_all(group, 'zh', 0, 0), 'core', axis=0, tiled=T...  6.93 us
    pallas_call x4, Pallas kernels, call(): pl.pallas_call(kernel, out_shape=outs, in_specs=in_specs, out_specs=jax.t...  4.22 us

profile of v8, /device:TPU:1, one launch (start us, length us, event | category | flops | bytes accessed | tf_op | source)
XLA Modules:
  0.0 97.6 jit_solution(13844999236882694929)
XLA Ops:
  0.6 0.0 copy-start
  0.6 0.0 copy-start.5
  0.7 0.0 copy-start.4
  0.7 0.0 copy-start.1
  0.7 0.0 copy-start.2
  0.7 0.8 fusion
  1.5 19.7 %all_to_all.25 = bf16[12,16,256]{2,1,0:T(8,128)(2,1)S(1)} all-to-all(bf16[12,16,256]{2,1,0:T(8,128)(2,1)S(1)} %broadcast_in_dim.6), channel_id=1, replica_groups=mesh['x'=4,'yh'=4,'yl'=2,'z'=3,'zh'=4,'core'=2] {'z','yh'}, dimensions={0} | all-to-all | bytes 196608 | tf_op jit(solution)/shard_map/all_to_all | solution.py:178
  21.3 0.1 broadcast_in_dim.7
  21.3 14.0 %all_to_all.26 = bf16[8,12,16,256]{3,2,1,0:T(8,128)(2,1)S(1)} all-to-all(bf16[8,12,16,256]{3,2,1,0:T(8,128)(2,1)S(1)} %broadcast_in_dim.7), channel_id=1, replica_groups=mesh['x'=4,'yh'=4,'yl'=2,'z'=3,'zh'=4,'core'=2] {'yl','x'}, dimensions={0} | all-to-all | bytes 1572864 | tf_op jit(solution)/shard_map/all_to_all | solution.py:178
  35.4 0.0 copy-done
  35.4 0.0 copy-done.5
  35.4 0.0 copy-done.4
  35.4 0.0 copy-done.1
  35.4 0.0 copy-done.2
  35.4 0.0 copy-start.3
  35.4 1.5 %shard_map.94 = bf16[4,80,256]{2,1,0:T(8,128)(2,1)S(1)} custom-call(s32[48]{0:T(128)S(1)} %copy-done.4, s32[48]{0:T(128)S(1)} %copy-done.5, bf16[48,128,128]{2,1,0:T(8,128)(2,1)S(1)} %copy-done, bf16[96,16,256]{2,1,0:T(8,128)(2,1)S(1)} %bitcast.7, bf16[16,256]{1,0:T(8,128)(2,1)S(1)} %copy-done.1, bf16[32,256]{1,0:T(8,128)(2,1)S(1)} %bitcast.8), custom_call_target="tpu_custom_call" | custom-call | tf_op jit(solution)/shard_map/pallas_call | solution.py:153
  36.9 23.9 %all_to_all.27 = bf16[4,80,256]{2,1,0:T(8,128)(2,1)S(1)} all-to-all(bf16[4,80,256]{2,1,0:T(8,128)(2,1)S(1)} %shard_map.94), channel_id=1, replica_groups=mesh['x'=4,'yh'=4,'yl'=2,'z'=3,'zh'=4,'core'=2] {'zh'}, dimensions={0} | all-to-all | bytes 327680 | tf_op jit(solution)/shard_map/all_to_all | solution.py:190
  60.8 6.9 %all_gather.3.group_ref = bf16[8,80,256]{2,1,0:T(8,128)(2,1)S(1)} all-gather(bf16[4,80,256]{2,1,0:T(8,128)(2,1)S(1)} %all_to_all.27), channel_id=1, replica_groups=mesh['x'=4,'yh'=4,'yl'=2,'z'=3,'zh'=4,'core'=2] {'core'}, dimensions={0}, use_global_device_ids=true | all-gather | bytes 491520 | tf_op jit(solution)/shard_map/all_gather | solution.py:190
  67.7 0.0 copy-done.3
  67.7 2.0 %shard_map.95 = (bf16[32,256]{1,0:T(8,128)(2,1)S(1)}, bf16[8,416,128]{2,1,0:T(8,128)(2,1)S(1)}) custom-call(s32[48]{0:T(128)S(1)} %copy-done.4, s32[48]{0:T(128)S(1)} %copy-done.5, bf16[48,128,128]{2,1,0:T(8,128)(2,1)S(1)} %copy-done, bf16[8,80,256]{2,1,0:T(8,128)(2,1)S(1)} %all_gather.3.group_ref, bf16[16,256]{1,0:T(8,128)(2,1)S(1)} %copy-done.1, ...), custom_call_target="tpu_custom_call" | custom-call | tf_op jit(solution)/shard_map/pallas_call | solution.py:153
  69.7 15.5 %all_to_all.28.got_ref = bf16[8,416,128]{2,1,0:T(8,128)(2,1)S(1)} all-to-all(bf16[8,416,128]{2,1,0:T(8,128)(2,1)S(1)} %get-tuple-element.8), channel_id=1, replica_groups=mesh['x'=4,'yh'=4,'yl'=2,'z'=3,'zh'=4,'core'=2] {'yl','x'}, dimensions={0} | all-to-all | bytes 1703936 | tf_op jit(solution)/shard_map/all_to_all | solution.py:211
  85.2 0.1 shard_map.96
  85.3 11.6 %all_to_all.29.got_ref = bf16[12,64,128]{2,1,0:T(8,128)(2,1)S(1)} all-to-all(bf16[12,64,128]{2,1,0:T(8,128)(2,1)S(1)} %shard_map.96), channel_id=1, replica_groups=mesh['x'=4,'yh'=4,'yl'=2,'z'=3,'zh'=4,'core'=2] {'z','yh'}, dimensions={0} | all-to-all | bytes 393216 | tf_op jit(solution)/shard_map/all_to_all | solution.py:218
  97.0 0.6 shard_map.97
  (1 shorter events, 0.0 us)
Async XLA Ops:
  0.6 34.7 %copy-start = (bf16[48,128,128]{2,1,0:T(8,128)(2,1)S(1)}, bf16[48,128,128]{2,1,0:T(8,128)(2,1)}, u32[]{:S(2)}) copy-start(bf16[48,128,128]{2,1,0:T(8,128)(2,1)} %tiles_ref.3) | copy-start | bytes 4718596
  0.6 34.7 %copy-start.5 = (s32[48]{0:T(128)S(1)}, s32[48]{0:T(128)}, u32[]{:S(2)}) copy-start(s32[48]{0:T(128)} %cols_ref.3) | copy-start | bytes 580
  0.7 34.7 %copy-start.4 = (s32[48]{0:T(128)S(1)}, s32[48]{0:T(128)}, u32[]{:S(2)}) copy-start(s32[48]{0:T(128)} %rows_ref.3) | copy-start | bytes 580
  0.7 34.7 %copy-start.1 = (bf16[16,256]{1,0:T(8,128)(2,1)S(1)}, bf16[16,256]{1,0:T(8,128)(2,1)}, u32[]{:S(2)}) copy-start(bf16[16,256]{1,0:T(8,128)(2,1)} %weight_ref.3) | copy-start | bytes 24580
  0.7 34.7 %copy-start.2 = (bf16[256,32]{0,1:T(8,128)(2,1)S(1)}, bf16[256,32]{0,1:T(8,128)(2,1)}, u32[]{:S(2)}) copy-start(bf16[256,32]{0,1:T(8,128)(2,1)} %param.13) | copy-start | bytes 49156
  35.4 32.3 %copy-start.3 = (f32[256]{0:T(256)S(1)}, f32[256]{0:T(256)}, u32[]{:S(2)}) copy-start(f32[256]{0:T(256)} %param.9) | copy-start | bytes 3076

commit v9 on v8

--- a/solution.py
+++ b/solution.py
@@ -2,6 +2,7 @@
 
 import jax
 import jax.numpy as jnp
+import numpy as np
 from jax import lax
 from jax.experimental import pallas as pl
 from jax.experimental.pallas import tpu as pltpu
@@ -24,25 +25,24 @@
     return lax.dot_general(left, right, dims, preferred_element_type=F32)
 
 
-def spot_of(tile, row_tiles, orders):
-    within, owner = lax.rem(tile, row_tiles), lax.div(tile, row_tiles)
-    where = {}
-    for axis in reversed(ROW):
-        where[axis], owner = lax.rem(owner, lax.axis_size(axis)), lax.div(owner, lax.axis_size(axis))
-    spot = 0
-    for axis in [axis for order in orders for axis in order]:
-        spot = spot * lax.axis_size(axis) + where[axis]
-    return spot, within
-
-
-def forward_kernel(rows_ref, cols_ref, tiles_ref, nodes_ref, weight_ref, cot_ref, out_ref):
+def spots(row_tiles):
+    sizes = [lax.axis_size(axis) for axis in ROW]
+    order = [ROW.index(axis) for axes in BACK for axis in axes]
+    owners = np.arange(np.prod(sizes)).reshape(sizes).transpose(order).reshape(-1)
+    table = np.empty((owners.size, row_tiles), np.int32)
+    table[owners] = np.arange(owners.size * row_tiles).reshape(-1, row_tiles)
+    return jnp.asarray(table.reshape(-1))
+
+
+def forward_kernel(rows_ref, cols_ref, spots_ref, tiles_ref, nodes_ref, weight_ref, cot_ref, out_ref):
     part = weight_ref.shape[0]
     row_tiles = cot_ref.shape[1] // LANES
     sums = jnp.zeros((row_tiles * part, LANES), F32)
     for t in range(0, tiles_ref.shape[0], 2):
         lefts = []
         for u in (t, t + 1):
-            owner, within = spot_of(cols_ref[u], row_tiles, OUT[::-1])
+            spot = spots_ref[cols_ref[u]]
+            owner, within = lax.div(spot, row_tiles), lax.rem(spot, row_tiles)
             nodes = nodes_ref[owner, :, pl.ds(pl.multiple_of(within * LANES, LANES), LANES)]
             none = jnp.zeros_like(nodes)
             lefts.append(
@@ -54,20 +54,16 @@
     for i in range(row_tiles):
         head, rest = halves(totals[i])
         cut = slice(i * LANES, (i + 1) * LANES)
-        for n in range(out_ref.shape[0]):
-            out_ref[n, 0:part, cut] = head
-            out_ref[n, part : 2 * part, cut] = rest
-    for n in range(out_ref.shape[0]):
-        out_ref[n, 2 * part : 3 * part] = weight_ref[...]
-        out_ref[n, 3 * part :] = cot_ref[...]
+        out_ref[0:part, cut] = head
+        out_ref[part : 2 * part, cut] = rest
+    out_ref[2 * part : 3 * part] = weight_ref[...]
+    out_ref[3 * part :] = cot_ref[...]
 
 
 def middle_kernel(
-    rows_ref, cols_ref, tiles_ref, group_ref, weight_ref, norm_ref, act_ref, out_ref, pre_ref, total_ref
+    rows_ref, cols_ref, spots_ref, tiles_ref, group_ref, weight_ref, norm_ref, act_ref, out_ref, pre_ref, total_ref
 ):
-    my_zh, my_core = lax.axis_index("zh"), lax.axis_index("core")
-    n_zh, n_core = lax.axis_size("zh"), lax.axis_size("core")
-    me, my_place = my_zh * n_core + my_core, my_core * n_zh + my_zh
+    me = lax.axis_index(FEAT)
     part = weight_ref.shape[0]
     hid_part = act_ref.shape[0]
     n_feat = group_ref.shape[0]
@@ -75,9 +71,7 @@
     head = group[:, 0:part].reshape(n_feat * part, -1)
     rest = group[:, part : 2 * part].reshape(n_feat * part, -1)
     weight_all = group[:, 2 * part : 3 * part].reshape(n_feat * part, -1)
-    cot = jnp.concatenate(
-        [group[core * n_zh + zh, 3 * part :] for zh in range(n_zh) for core in range(n_core)], axis=0
-    )
+    cot = group[:, 3 * part :].reshape(n_feat * hid_part, -1)
     norm = norm_ref[...]
     pre = (dot(weight_all, head, TN) + dot(weight_all, rest, TN)) * norm
     pre_ref[...] = pre
@@ -100,11 +94,10 @@
         for i in range(1, row_tiles):
             left = jnp.where(rows_ref[t] == i, back_tiles[i], left)
         both = dot(left, tiles_ref[t], NN)
-        owner, within = spot_of(cols_ref[t], row_tiles, BACK)
-        total_ref[owner * row_tiles + within] += both[:part] + both[part:]
-
-    own_head = group_ref[pl.ds(my_place, 1), 0:part][0]
-    own_rest = group_ref[pl.ds(my_place, 1), part : 2 * part][0]
+        total_ref[spots_ref[cols_ref[t]]] += both[:part] + both[part:]
+
+    own_head = group_ref[pl.ds(me, 1), 0:part][0]
+    own_rest = group_ref[pl.ds(me, 1), part : 2 * part][0]
     weight_part = dot(own_head, back_in, NT) + dot(own_rest, back_in, NT)
     n_first, n_rows, _ = out_ref.shape
     cols = total_ref.shape[0] // n_first
@@ -171,6 +164,7 @@
     col_tiles = n_first * n_second * row_tiles
     norm = norm_scale.reshape(1, rows_dev)
     shape = jax.ShapeDtypeStruct
+    table = spots(row_tiles)
 
     block = (features.T.astype(F32) * norm_scale[None, :]).astype(BF16)
     for axes in OUT:
@@ -178,16 +172,17 @@
         block = lax.all_to_all(block, axes, 0, 0)
     group = call(
         forward_kernel,
-        shape((lax.axis_size("zh"), 3 * part + hid_part, rows_dev), BF16),
-        [SMEM, SMEM, VMEM, VMEM, VMEM, VMEM],
+        shape((3 * part + hid_part, rows_dev), BF16),
+        [SMEM, SMEM, SMEM, VMEM, VMEM, VMEM, VMEM],
         tile_rows,
         tile_cols,
+        table,
         tile_vals,
         block.reshape(n_first * n_second, part, rows_dev),
         weight,
         cotangent.T,
     )
-    group = lax.all_gather(lax.all_to_all(group, "zh", 0, 0), "core", axis=0, tiled=True)
+    group = lax.all_gather(group, FEAT)
     own = row_tiles * part
     weight_rows = part * hidden // tile_len
     activated, sent = call(
@@ -196,9 +191,10 @@
             shape((hid_part, rows_dev), BF16),
             shape((n_first, n_second * own + weight_rows, tile_len), BF16),
         ),
-        [SMEM, SMEM, VMEM, VMEM, VMEM, VMEM],
+        [SMEM, SMEM, SMEM, VMEM, VMEM, VMEM, VMEM],
         tile_rows,
         tile_cols,
+        table,
         tile_vals,
         group,
         weight,

time: 98.6 us -> 96.5 us (0.979)
    all_to_all x1 -> x0, blocking collectives: 23.9 us -> none  [per_device(): lax.all_to_all(group, 'zh', 0, 0)]
    all_gather x1, blocking collectives: 6.93 us -> 29.6 us  [per_device(): group = lax.all_gather(group, FEAT)]
where the time goes in v9:
time: 96.5 us; the launch traced here: 96.2 us
  blocking collectives  90.9 us (94%)
  Pallas kernels  3.67 us (4%)
    all_to_all x2, blocking collectives, per_device(): block = lax.all_to_all(block, axes, 0, 0)  33.8 us
    all_gather x1, blocking collectives, per_device(): group = lax.all_gather(group, FEAT)  29.6 us
    all_to_all x1, blocking collectives, per_device(): got = lax.all_to_all(sent, BACK[0], 0, 0)  15.6 us
    all_to_all x1, blocking collectives, per_device(): got = lax.all_to_all(sent, BACK[1], 0, 0)  12 us
    pallas_call x4, Pallas kernels, call(): pl.pallas_call(kernel, out_shape=outs, in_specs=in_specs, out_specs=jax.t...  3.67 us

profile of v9, /device:TPU:1, one launch (start us, length us, event | category | flops | bytes accessed | tf_op | source)
XLA Modules:
  0.0 96.2 jit_solution(9017863089592357030)
XLA Ops:
  0.6 0.0 copy-start.4
  0.6 0.0 copy-start
  0.7 0.0 copy-start.6
  0.7 0.0 copy-start.5
  0.7 0.0 copy-start.1
  0.7 0.0 copy-start.2
  0.7 0.8 fusion
  1.5 19.7 %all_to_all.20 = bf16[12,16,256]{2,1,0:T(8,128)(2,1)S(1)} all-to-all(bf16[12,16,256]{2,1,0:T(8,128)(2,1)S(1)} %broadcast_in_dim.6), channel_id=1, replica_groups=mesh['x'=4,'yh'=4,'yl'=2,'z'=3,'zh'=4,'core'=2] {'z','yh'}, dimensions={0} | all-to-all | bytes 196608 | tf_op jit(solution)/shard_map/all_to_all | solution.py:172
  21.3 0.1 broadcast_in_dim.7
  21.3 14.0 %all_to_all.21 = bf16[8,12,16,256]{3,2,1,0:T(8,128)(2,1)S(1)} all-to-all(bf16[8,12,16,256]{3,2,1,0:T(8,128)(2,1)S(1)} %broadcast_in_dim.7), channel_id=1, replica_groups=mesh['x'=4,'yh'=4,'yl'=2,'z'=3,'zh'=4,'core'=2] {'yl','x'}, dimensions={0} | all-to-all | bytes 1572864 | tf_op jit(solution)/shard_map/all_to_all | solution.py:172
  35.4 0.0 copy-start.3
  35.4 0.0 copy-done.4
  35.4 0.0 copy-done
  35.4 0.0 copy-done.6
  35.4 0.0 copy-done.5
  35.4 0.0 copy-done.1
  35.4 0.0 copy-done.2
  35.4 1.2 %shard_map.103 = bf16[80,256]{1,0:T(8,128)(2,1)S(1)} custom-call(s32[48]{0:T(128)S(1)} %copy-done.5, s32[48]{0:T(128)S(1)} %copy-done.6, s32[192]{0:T(256)S(1)} %copy-done.4, bf16[48,128,128]{2,1,0:T(8,128)(2,1)S(1)} %copy-done, bf16[96,16,256]{2,1,0:T(8,128)(2,1)S(1)} %bitcast.8, bf16[16,256]{1,0:T(8,128)(2,1)S(1)} %copy-done.1, bf16[32,256]{1,0:T(8,128)(2,1)S(1)} %bitcast.10), custom_call_target="tpu_custom_call" | custom-call | tf_op jit(solution)/shard_map/pallas_call | solution.py:146
  36.6 29.6 %all-gather = bf16[640,256]{1,0:T(8,128)(2,1)S(1)} all-gather(bf16[80,256]{1,0:T(8,128)(2,1)S(1)} %shard_map.103), channel_id=2, replica_groups=mesh['x'=4,'yh'=4,'yl'=2,'z'=3,'zh'=4,'core'=2] {'zh','core'}, dimensions={0}, use_global_device_ids=true | all-gather | bytes 368640 | tf_op jit(solution)/shard_map/all_gather | solution.py:185
  66.2 0.0 copy-done.3
  66.2 1.7 %shard_map.104 = (bf16[32,256]{1,0:T(8,128)(2,1)S(1)}, bf16[8,416,128]{2,1,0:T(8,128)(2,1)S(1)}) custom-call(s32[48]{0:T(128)S(1)} %copy-done.5, s32[48]{0:T(128)S(1)} %copy-done.6, s32[192]{0:T(256)S(1)} %copy-done.4, bf16[48,128,128]{2,1,0:T(8,128)(2,1)S(1)} %copy-done, bf16[8,80,256]{2,1,0:T(8,128)(2,1)S(1)} %bitcast.9, bf16[16,256]{1,0:T(8,128)(2,1)S(1)} %copy-done.1, ...), custom_call_target="tpu_custom_call" | custom-call | tf_op jit(solution)/shard_map/pallas_call | solution.py:146
  67.9 15.6 %all_to_all.22.got_ref = bf16[8,416,128]{2,1,0:T(8,128)(2,1)S(1)} all-to-all(bf16[8,416,128]{2,1,0:T(8,128)(2,1)S(1)} %get-tuple-element.8), channel_id=1, replica_groups=mesh['x'=4,'yh'=4,'yl'=2,'z'=3,'zh'=4,'core'=2] {'yl','x'}, dimensions={0} | all-to-all | bytes 1703936 | tf_op jit(solution)/shard_map/all_to_all | solution.py:207
  83.5 0.1 shard_map.105
  83.6 12.0 %all_to_all.23.got_ref = bf16[12,64,128]{2,1,0:T(8,128)(2,1)S(1)} all-to-all(bf16[12,64,128]{2,1,0:T(8,128)(2,1)S(1)} %shard_map.105), channel_id=1, replica_groups=mesh['x'=4,'yh'=4,'yl'=2,'z'=3,'zh'=4,'core'=2] {'z','yh'}, dimensions={0} | all-to-all | bytes 393216 | tf_op jit(solution)/shard_map/all_to_all | solution.py:214
  95.6 0.6 shard_map.106
  (1 shorter events, 0.0 us)
Async XLA Ops:
  0.6 34.7 %copy-start.4 = (s32[192]{0:T(256)S(1)}, s32[192]{0:T(256)}, u32[]{:S(2)}) copy-start(s32[192]{0:T(256)} %constant.2.clone.spots_ref) | copy-start | bytes 2308
  0.6 34.7 %copy-start = (bf16[48,128,128]{2,1,0:T(8,128)(2,1)S(1)}, bf16[48,128,128]{2,1,0:T(8,128)(2,1)}, u32[]{:S(2)}) copy-start(bf16[48,128,128]{2,1,0:T(8,128)(2,1)} %tiles_ref.3) | copy-start | bytes 4718596
  0.7 34.7 %copy-start.6 = (s32[48]{0:T(128)S(1)}, s32[48]{0:T(128)}, u32[]{:S(2)}) copy-start(s32[48]{0:T(128)} %cols_ref.3) | copy-start | bytes 580
  0.7 34.7 %copy-start.5 = (s32[48]{0:T(128)S(1)}, s32[48]{0:T(128)}, u32[]{:S(2)}) copy-start(s32[48]{0:T(128)} %rows_ref.3) | copy-start | bytes 580
  0.7 34.7 %copy-start.1 = (bf16[16,256]{1,0:T(8,128)(2,1)S(1)}, bf16[16,256]{1,0:T(8,128)(2,1)}, u32[]{:S(2)}) copy-start(bf16[16,256]{1,0:T(8,128)(2,1)} %weight_ref.3) | copy-start | bytes 24580
  0.7 34.7 %copy-start.2 = (bf16[256,32]{0,1:T(8,128)(2,1)S(1)}, bf16[256,32]{0,1:T(8,128)(2,1)}, u32[]{:S(2)}) copy-start(bf16[256,32]{0,1:T(8,128)(2,1)} %param.14) | copy-start | bytes 49156
  35.4 30.8 %copy-start.3 = (f32[256]{0:T(256)S(1)}, f32[256]{0:T(256)}, u32[]{:S(2)}) copy-start(f32[256]{0:T(256)} %param.10) | copy-start | bytes 3076

commit v10 on v9

--- a/solution.py
+++ b/solution.py
@@ -34,9 +34,23 @@
     return jnp.asarray(table.reshape(-1))
 
 
-def forward_kernel(rows_ref, cols_ref, spots_ref, tiles_ref, nodes_ref, weight_ref, cot_ref, out_ref):
+def index_copies(sources, targets, sems):
+    copies = [pltpu.make_async_copy(s, t, sems.at[i]) for i, (s, t) in enumerate(zip(sources, targets))]
+    for copy in copies:
+        copy.start()
+    return copies
+
+
+def forward_kernel(
+    rows_in, cols_in, spots_in, tiles_ref, nodes_ref, weight_ref, cot_ref, out_ref, rows_ref, cols_ref, spots_ref, sems
+):
+    copies = index_copies((rows_in, cols_in, spots_in), (rows_ref, cols_ref, spots_ref), sems)
     part = weight_ref.shape[0]
     row_tiles = cot_ref.shape[1] // LANES
+    out_ref[2 * part : 3 * part] = weight_ref[...]
+    out_ref[3 * part :] = cot_ref[...]
+    for copy in copies:
+        copy.wait()
     sums = jnp.zeros((row_tiles * part, LANES), F32)
     for t in range(0, tiles_ref.shape[0], 2):
         lefts = []
@@ -56,13 +70,26 @@
         cut = slice(i * LANES, (i + 1) * LANES)
         out_ref[0:part, cut] = head
         out_ref[part : 2 * part, cut] = rest
-    out_ref[2 * part : 3 * part] = weight_ref[...]
-    out_ref[3 * part :] = cot_ref[...]
 
 
 def middle_kernel(
-    rows_ref, cols_ref, spots_ref, tiles_ref, group_ref, weight_ref, norm_ref, act_ref, out_ref, pre_ref, total_ref
+    rows_in,
+    cols_in,
+    spots_in,
+    tiles_ref,
+    group_ref,
+    weight_ref,
+    norm_ref,
+    act_ref,
+    out_ref,
+    pre_ref,
+    total_ref,
+    rows_ref,
+    cols_ref,
+    spots_ref,
+    sems,
 ):
+    copies = index_copies((rows_in, cols_in, spots_in), (rows_ref, cols_ref, spots_ref), sems)
     me = lax.axis_index(FEAT)
     part = weight_ref.shape[0]
     hid_part = act_ref.shape[0]
@@ -73,7 +100,7 @@
     weight_all = group[:, 2 * part : 3 * part].reshape(n_feat * part, -1)
     cot = group[:, 3 * part :].reshape(n_feat * hid_part, -1)
     norm = norm_ref[...]
-    pre = (dot(weight_all, head, TN) + dot(weight_all, rest, TN)) * norm
+    pre = dot(jnp.concatenate([weight_all] * 2, axis=0), jnp.concatenate([head, rest], axis=0), TN) * norm
     pre_ref[...] = pre
     sigma = 1.0 / (1.0 + jnp.exp(-pre))
     slope = sigma * (1.0 + pre * (1.0 - sigma))
@@ -84,21 +111,26 @@
     back = dot(weight_ref[...], back_in, NN)
     row_tiles = back.shape[1] // LANES
     back_head, back_rest = halves(back)
-    back_tiles = [
-        jnp.concatenate([h[:, i * LANES : (i + 1) * LANES] for h in (back_head, back_rest)], axis=0)
-        for i in range(row_tiles)
-    ]
+    left = jnp.concatenate(
+        [h[:, i * LANES : (i + 1) * LANES] for i in range(row_tiles) for h in (back_head, back_rest)],
+        axis=0,
+    )
     total_ref[...] = jnp.zeros_like(total_ref)
-    for t in range(tiles_ref.shape[0]):
-        left = back_tiles[0]
-        for i in range(1, row_tiles):
-            left = jnp.where(rows_ref[t] == i, back_tiles[i], left)
-        both = dot(left, tiles_ref[t], NN)
-        total_ref[spots_ref[cols_ref[t]]] += both[:part] + both[part:]
-
-    own_head = group_ref[pl.ds(me, 1), 0:part][0]
-    own_rest = group_ref[pl.ds(me, 1), part : 2 * part][0]
-    weight_part = dot(own_head, back_in, NT) + dot(own_rest, back_in, NT)
+    for copy in copies:
+        copy.wait()
+    for t in range(0, tiles_ref.shape[0], 2):
+        wide = dot(left, jnp.concatenate([tiles_ref[t], tiles_ref[t + 1]], axis=1), NN)
+        wide = wide.reshape(row_tiles, 2, part, -1)
+        wide = [wide[i, 0] + wide[i, 1] for i in range(row_tiles)]
+        for k in range(2):
+            cut = slice(k * LANES, (k + 1) * LANES)
+            term = wide[0][:, cut]
+            for i in range(1, row_tiles):
+                term = jnp.where(rows_ref[t + k] == i, wide[i][:, cut], term)
+            total_ref[spots_ref[cols_ref[t + k]]] += term
+
+    own = dot(group_ref[pl.ds(me, 1), 0 : 2 * part][0], back_in, NT)
+    weight_part = own[:part] + own[part:]
     n_first, n_rows, _ = out_ref.shape
     cols = total_ref.shape[0] // n_first
     total = total_ref[...].astype(BF16).reshape(n_first, cols * part, LANES)
@@ -137,7 +169,6 @@
         spot += part
 
 
-SMEM = pl.BlockSpec(memory_space=pltpu.SMEM)
 VMEM = pl.BlockSpec(memory_space=pltpu.VMEM)
 SCOPED = pltpu.CompilerParams(vmem_limit_bytes=24 * 2**20)
 
@@ -165,6 +196,8 @@
     norm = norm_scale.reshape(1, rows_dev)
     shape = jax.ShapeDtypeStruct
     table = spots(row_tiles)
+    indices = tuple(pltpu.SMEM(a.shape, jnp.int32) for a in (tile_rows, tile_cols, table))
+    indices += (pltpu.SemaphoreType.DMA((3,)),)
 
     block = (features.T.astype(F32) * norm_scale[None, :]).astype(BF16)
     for axes in OUT:
@@ -173,7 +206,7 @@
     group = call(
         forward_kernel,
         shape((3 * part + hid_part, rows_dev), BF16),
-        [SMEM, SMEM, SMEM, VMEM, VMEM, VMEM, VMEM],
+        [VMEM, VMEM, VMEM, VMEM, VMEM, VMEM, VMEM],
         tile_rows,
         tile_cols,
         table,
@@ -181,6 +214,7 @@
         block.reshape(n_first * n_second, part, rows_dev),
         weight,
         cotangent.T,
+        scratch=indices,
     )
     group = lax.all_gather(group, FEAT)
     own = row_tiles * part
@@ -191,7 +225,7 @@
             shape((hid_part, rows_dev), BF16),
             shape((n_first, n_second * own + weight_rows, tile_len), BF16),
         ),
-        [SMEM, SMEM, SMEM, VMEM, VMEM, VMEM, VMEM],
+        [VMEM, VMEM, VMEM, VMEM, VMEM, VMEM, VMEM],
         tile_rows,
         tile_cols,
         table,
@@ -202,7 +236,8 @@
         scratch=(
             pltpu.VMEM((hidden, rows_dev), F32),
             pltpu.VMEM((col_tiles, part, tile_len), F32),
-        ),
+        )
+        + indices,
     )
     got = lax.all_to_all(sent, BACK[0], 0, 0)
     sent = call(

time: 96.5 us -> 96.2 us (level)
  no operation moved by 1% of the time
where the time goes in v10:
time: 96.2 us; the launch traced here: 96 us
  blocking collectives  90.9 us (94%)
  Pallas kernels  3.38 us (4%)
    all_to_all x2, blocking collectives, per_device(): block = lax.all_to_all(block, axes, 0, 0)  33.8 us
    all_gather x1, blocking collectives, per_device(): group = lax.all_gather(group, FEAT)  29.6 us
    all_to_all x1, blocking collectives, per_device(): got = lax.all_to_all(sent, BACK[0], 0, 0)  15.6 us
    all_to_all x1, blocking collectives, per_device(): got = lax.all_to_all(sent, BACK[1], 0, 0)  12 us
    pallas_call x4, Pallas kernels, call(): pl.pallas_call(kernel, out_shape=outs, in_specs=in_specs, out_specs=jax.t...  3.38 us

profile of v10, /device:TPU:1, one launch (start us, length us, event | category | flops | bytes accessed | tf_op | source)
XLA Modules:
  0.0 96.0 jit_solution(17781781275867114254)
XLA Ops:
  0.6 0.0 copy-start.4
  0.6 0.0 copy-start
  0.7 0.0 copy-start.6
  0.7 0.0 copy-start.5
  0.7 0.0 copy-start.1
  0.7 0.0 copy-start.2
  0.7 0.8 fusion
  1.5 19.7 %all_to_all.20 = bf16[12,16,256]{2,1,0:T(8,128)(2,1)S(1)} all-to-all(bf16[12,16,256]{2,1,0:T(8,128)(2,1)S(1)} %broadcast_in_dim.6), channel_id=1, replica_groups=mesh['x'=4,'yh'=4,'yl'=2,'z'=3,'zh'=4,'core'=2] {'z','yh'}, dimensions={0} | all-to-all | bytes 196608 | tf_op jit(solution)/shard_map/all_to_all | solution.py:205
  21.3 0.1 broadcast_in_dim.7
  21.3 14.0 %all_to_all.21 = bf16[8,12,16,256]{3,2,1,0:T(8,128)(2,1)S(1)} all-to-all(bf16[8,12,16,256]{3,2,1,0:T(8,128)(2,1)S(1)} %broadcast_in_dim.7), channel_id=1, replica_groups=mesh['x'=4,'yh'=4,'yl'=2,'z'=3,'zh'=4,'core'=2] {'yl','x'}, dimensions={0} | all-to-all | bytes 1572864 | tf_op jit(solution)/shard_map/all_to_all | solution.py:205
  35.4 0.0 copy-start.3
  35.4 0.0 copy-done.4
  35.4 0.0 copy-done
  35.4 0.0 copy-done.6
  35.4 0.0 copy-done.5
  35.4 0.0 copy-done.1
  35.4 0.0 copy-done.2
  35.4 1.2 %shard_map.103 = bf16[80,256]{1,0:T(8,128)(2,1)S(1)} custom-call(s32[48]{0:T(128)S(1)} %copy-done.5, s32[48]{0:T(128)S(1)} %copy-done.6, s32[192]{0:T(256)S(1)} %copy-done.4, bf16[48,128,128]{2,1,0:T(8,128)(2,1)S(1)} %copy-done, bf16[96,16,256]{2,1,0:T(8,128)(2,1)S(1)} %bitcast.8, bf16[16,256]{1,0:T(8,128)(2,1)S(1)} %copy-done.1, bf16[32,256]{1,0:T(8,128)(2,1)S(1)} %bitcast.10), custom_call_target="tpu_custom_call" | custom-call | tf_op jit(solution)/shard_map/pallas_call | solution.py:177
  36.6 29.6 %all-gather = bf16[640,256]{1,0:T(8,128)(2,1)S(1)} all-gather(bf16[80,256]{1,0:T(8,128)(2,1)S(1)} %shard_map.103), channel_id=2, replica_groups=mesh['x'=4,'yh'=4,'yl'=2,'z'=3,'zh'=4,'core'=2] {'zh','core'}, dimensions={0}, use_global_device_ids=true | all-gather | bytes 368640 | tf_op jit(solution)/shard_map/all_gather | solution.py:219
  66.2 0.0 copy-done.3
  66.2 1.4 %shard_map.104 = (bf16[32,256]{1,0:T(8,128)(2,1)S(1)}, bf16[8,416,128]{2,1,0:T(8,128)(2,1)S(1)}) custom-call(s32[48]{0:T(128)S(1)} %copy-done.5, s32[48]{0:T(128)S(1)} %copy-done.6, s32[192]{0:T(256)S(1)} %copy-done.4, bf16[48,128,128]{2,1,0:T(8,128)(2,1)S(1)} %copy-done, bf16[8,80,256]{2,1,0:T(8,128)(2,1)S(1)} %bitcast.9, bf16[16,256]{1,0:T(8,128)(2,1)S(1)} %copy-done.1, ...), custom_call_target="tpu_custom_call" | custom-call | tf_op jit(solution)/shard_map/pallas_call | solution.py:177
  67.6 15.6 %all_to_all.22.got_ref = bf16[8,416,128]{2,1,0:T(8,128)(2,1)S(1)} all-to-all(bf16[8,416,128]{2,1,0:T(8,128)(2,1)S(1)} %get-tuple-element.8), channel_id=1, replica_groups=mesh['x'=4,'yh'=4,'yl'=2,'z'=3,'zh'=4,'core'=2] {'yl','x'}, dimensions={0} | all-to-all | bytes 1703936 | tf_op jit(solution)/shard_map/all_to_all | solution.py:242
  83.2 0.1 shard_map.105
  83.4 12.0 %all_to_all.23.got_ref = bf16[12,64,128]{2,1,0:T(8,128)(2,1)S(1)} all-to-all(bf16[12,64,128]{2,1,0:T(8,128)(2,1)S(1)} %shard_map.105), channel_id=1, replica_groups=mesh['x'=4,'yh'=4,'yl'=2,'z'=3,'zh'=4,'core'=2] {'z','yh'}, dimensions={0} | all-to-all | bytes 393216 | tf_op jit(solution)/shard_map/all_to_all | solution.py:249
  95.3 0.6 shard_map.106
  (1 shorter events, 0.0 us)
Async XLA Ops:
  0.6 34.7 %copy-start.4 = (s32[192]{0:T(256)S(1)}, s32[192]{0:T(256)}, u32[]{:S(2)}) copy-start(s32[192]{0:T(256)} %constant.2.clone.spots_in) | copy-start | bytes 2308
  0.6 34.7 %copy-start = (bf16[48,128,128]{2,1,0:T(8,128)(2,1)S(1)}, bf16[48,128,128]{2,1,0:T(8,128)(2,1)}, u32[]{:S(2)}) copy-start(bf16[48,128,128]{2,1,0:T(8,128)(2,1)} %tiles_ref.3) | copy-start | bytes 4718596
  0.7 34.7 %copy-start.6 = (s32[48]{0:T(128)S(1)}, s32[48]{0:T(128)}, u32[]{:S(2)}) copy-start(s32[48]{0:T(128)} %cols_in.3) | copy-start | bytes 580
  0.7 34.7 %copy-start.5 = (s32[48]{0:T(128)S(1)}, s32[48]{0:T(128)}, u32[]{:S(2)}) copy-start(s32[48]{0:T(128)} %rows_in.3) | copy-start | bytes 580
  0.7 34.7 %copy-start.1 = (bf16[16,256]{1,0:T(8,128)(2,1)S(1)}, bf16[16,256]{1,0:T(8,128)(2,1)}, u32[]{:S(2)}) copy-start(bf16[16,256]{1,0:T(8,128)(2,1)} %weight_ref.3) | copy-start | bytes 24580
  0.7 34.7 %copy-start.2 = (bf16[256,32]{0,1:T(8,128)(2,1)S(1)}, bf16[256,32]{0,1:T(8,128)(2,1)}, u32[]{:S(2)}) copy-start(bf16[256,32]{0,1:T(8,128)(2,1)} %param.14) | copy-start | bytes 49156
  35.4 30.8 %copy-start.3 = (f32[256]{0:T(256)S(1)}, f32[256]{0:T(256)}, u32[]{:S(2)}) copy-start(f32[256]{0:T(256)} %param.10) | copy-start | bytes 3076

commit v11 on v10

--- a/solution.py
+++ b/solution.py
@@ -42,13 +42,13 @@
 
 
 def forward_kernel(
-    rows_in, cols_in, spots_in, tiles_ref, nodes_ref, weight_ref, cot_ref, out_ref, rows_ref, cols_ref, spots_ref, sems
+    rows_in, cols_in, spots_in, tiles_ref, nodes_ref, weight_ref, cot_ref, out_ref, own_ref, rows_ref, cols_ref, spots_ref, sems
 ):
     copies = index_copies((rows_in, cols_in, spots_in), (rows_ref, cols_ref, spots_ref), sems)
     part = weight_ref.shape[0]
     row_tiles = cot_ref.shape[1] // LANES
-    out_ref[2 * part : 3 * part] = weight_ref[...]
-    out_ref[3 * part :] = cot_ref[...]
+    out_ref[part : 2 * part] = weight_ref[...]
+    out_ref[2 * part :] = cot_ref[...]
     for copy in copies:
         copy.wait()
     sums = jnp.zeros((row_tiles * part, LANES), F32)
@@ -69,7 +69,8 @@
         head, rest = halves(totals[i])
         cut = slice(i * LANES, (i + 1) * LANES)
         out_ref[0:part, cut] = head
-        out_ref[part : 2 * part, cut] = rest
+        own_ref[0:part, cut] = head
+        own_ref[part:, cut] = rest
 
 
 def middle_kernel(
@@ -78,6 +79,7 @@
     spots_in,
     tiles_ref,
     group_ref,
+    own_ref,
     weight_ref,
     norm_ref,
     act_ref,
@@ -96,11 +98,10 @@
     n_feat = group_ref.shape[0]
     group = group_ref[...]
     head = group[:, 0:part].reshape(n_feat * part, -1)
-    rest = group[:, part : 2 * part].reshape(n_feat * part, -1)
-    weight_all = group[:, 2 * part : 3 * part].reshape(n_feat * part, -1)
-    cot = group[:, 3 * part :].reshape(n_feat * hid_part, -1)
+    weight_all = group[:, part : 2 * part].reshape(n_feat * part, -1)
+    cot = group[:, 2 * part :].reshape(n_feat * hid_part, -1)
     norm = norm_ref[...]
-    pre = dot(jnp.concatenate([weight_all] * 2, axis=0), jnp.concatenate([head, rest], axis=0), TN) * norm
+    pre = dot(weight_all, head, TN) * norm
     pre_ref[...] = pre
     sigma = 1.0 / (1.0 + jnp.exp(-pre))
     slope = sigma * (1.0 + pre * (1.0 - sigma))
@@ -129,7 +130,7 @@
                 term = jnp.where(rows_ref[t + k] == i, wide[i][:, cut], term)
             total_ref[spots_ref[cols_ref[t + k]]] += term
 
-    own = dot(group_ref[pl.ds(me, 1), 0 : 2 * part][0], back_in, NT)
+    own = dot(own_ref[...], back_in, NT)
     weight_part = own[:part] + own[part:]
     n_first, n_rows, _ = out_ref.shape
     cols = total_ref.shape[0] // n_first
@@ -203,9 +204,9 @@
     for axes in OUT:
         block = jnp.broadcast_to(block[None], (lax.axis_size(axes),) + block.shape)
         block = lax.all_to_all(block, axes, 0, 0)
-    group = call(
+    group, own_mixed = call(
         forward_kernel,
-        shape((3 * part + hid_part, rows_dev), BF16),
+        (shape((2 * part + hid_part, rows_dev), BF16), shape((2 * part, rows_dev), BF16)),
         [VMEM, VMEM, VMEM, VMEM, VMEM, VMEM, VMEM],
         tile_rows,
         tile_cols,
@@ -225,12 +226,13 @@
             shape((hid_part, rows_dev), BF16),
             shape((n_first, n_second * own + weight_rows, tile_len), BF16),
         ),
-        [VMEM, VMEM, VMEM, VMEM, VMEM, VMEM, VMEM],
+        [VMEM] * 8,
         tile_rows,
         tile_cols,
         table,
         tile_vals,
         group,
+        own_mixed,
         weight,
         norm,
         scratch=(

time: 96.2 us -> 95.7 us (level)
  no operation moved by 1% of the time
where the time goes in v11:
time: 95.7 us; the launch traced here: 95.4 us
  blocking collectives  90.4 us (94%)
  Pallas kernels  3.4 us (4%)
    all_to_all x2, blocking collectives, per_device(): block = lax.all_to_all(block, axes, 0, 0)  33.8 us
    all_gather x1, blocking collectives, per_device(): group = lax.all_gather(group, FEAT)  29 us
    all_to_all x1, blocking collectives, per_device(): got = lax.all_to_all(sent, BACK[0], 0, 0)  15.6 us
    all_to_all x1, blocking collectives, per_device(): got = lax.all_to_all(sent, BACK[1], 0, 0)  11.9 us
    pallas_call x4, Pallas kernels, call(): pl.pallas_call(kernel, out_shape=outs, in_specs=in_specs, out_specs=jax.t...  3.4 us

profile of v11, /device:TPU:1, one launch (start us, length us, event | category | flops | bytes accessed | tf_op | source)
XLA Modules:
  0.0 95.4 jit_solution(11756095234199346943)
XLA Ops:
  0.6 0.0 copy-start.4
  0.6 0.0 copy-start
  0.7 0.0 copy-start.6
  0.7 0.0 copy-start.5
  0.7 0.0 copy-start.1
  0.7 0.0 copy-start.2
  0.7 0.8 fusion
  1.5 19.7 %all_to_all.20 = bf16[12,16,256]{2,1,0:T(8,128)(2,1)S(1)} all-to-all(bf16[12,16,256]{2,1,0:T(8,128)(2,1)S(1)} %broadcast_in_dim.6), channel_id=1, replica_groups=mesh['x'=4,'yh'=4,'yl'=2,'z'=3,'zh'=4,'core'=2] {'z','yh'}, dimensions={0} | all-to-all | bytes 196608 | tf_op jit(solution)/shard_map/all_to_all | solution.py:206
  21.3 0.1 broadcast_in_dim.7
  21.3 14.0 %all_to_all.21 = bf16[8,12,16,256]{3,2,1,0:T(8,128)(2,1)S(1)} all-to-all(bf16[8,12,16,256]{3,2,1,0:T(8,128)(2,1)S(1)} %broadcast_in_dim.7), channel_id=1, replica_groups=mesh['x'=4,'yh'=4,'yl'=2,'z'=3,'zh'=4,'core'=2] {'yl','x'}, dimensions={0} | all-to-all | bytes 1572864 | tf_op jit(solution)/shard_map/all_to_all | solution.py:206
  35.4 0.0 copy-start.3
  35.4 0.0 copy-done.4
  35.4 0.0 copy-done
  35.4 0.0 copy-done.6
  35.4 0.0 copy-done.5
  35.4 0.0 copy-done.1
  35.4 0.0 copy-done.2
  35.4 1.2 %shard_map.103 = (bf16[64,256]{1,0:T(8,128)(2,1)S(1)}, bf16[32,256]{1,0:T(8,128)(2,1)S(1)}) custom-call(s32[48]{0:T(128)S(1)} %copy-done.5, s32[48]{0:T(128)S(1)} %copy-done.6, s32[192]{0:T(256)S(1)} %copy-done.4, bf16[48,128,128]{2,1,0:T(8,128)(2,1)S(1)} %copy-done, bf16[96,16,256]{2,1,0:T(8,128)(2,1)S(1)} %bitcast.8, bf16[16,256]{1,0:T(8,128)(2,1)S(1)} %copy-done.1, ...), custom_call_target="tpu_custom_call" | custom-call | tf_op jit(solution)/shard_map/pallas_call | solution.py:178
  36.6 29.0 %all-gather = bf16[512,256]{1,0:T(8,128)(2,1)S(1)} all-gather(bf16[64,256]{1,0:T(8,128)(2,1)S(1)} %get-tuple-element.10), channel_id=2, replica_groups=mesh['x'=4,'yh'=4,'yl'=2,'z'=3,'zh'=4,'core'=2] {'zh','core'}, dimensions={0}, use_global_device_ids=true | all-gather | bytes 294912 | tf_op jit(solution)/shard_map/all_gather | solution.py:220
  65.7 0.0 copy-done.3
  65.7 1.4 %shard_map.104 = (bf16[32,256]{1,0:T(8,128)(2,1)S(1)}, bf16[8,416,128]{2,1,0:T(8,128)(2,1)S(1)}) custom-call(s32[48]{0:T(128)S(1)} %copy-done.5, s32[48]{0:T(128)S(1)} %copy-done.6, s32[192]{0:T(256)S(1)} %copy-done.4, bf16[48,128,128]{2,1,0:T(8,128)(2,1)S(1)} %copy-done, bf16[8,64,256]{2,1,0:T(8,128)(2,1)S(1)} %bitcast.9, ...), custom_call_target="tpu_custom_call" | custom-call | tf_op jit(solution)/shard_map/pallas_call | solution.py:178
  67.1 15.6 %all_to_all.22.got_ref = bf16[8,416,128]{2,1,0:T(8,128)(2,1)S(1)} all-to-all(bf16[8,416,128]{2,1,0:T(8,128)(2,1)S(1)} %get-tuple-element.12), channel_id=1, replica_groups=mesh['x'=4,'yh'=4,'yl'=2,'z'=3,'zh'=4,'core'=2] {'yl','x'}, dimensions={0} | all-to-all | bytes 1703936 | tf_op jit(solution)/shard_map/all_to_all | solution.py:244
  82.7 0.1 shard_map.105
  82.8 11.9 %all_to_all.23.got_ref = bf16[12,64,128]{2,1,0:T(8,128)(2,1)S(1)} all-to-all(bf16[12,64,128]{2,1,0:T(8,128)(2,1)S(1)} %shard_map.105), channel_id=1, replica_groups=mesh['x'=4,'yh'=4,'yl'=2,'z'=3,'zh'=4,'core'=2] {'z','yh'}, dimensions={0} | all-to-all | bytes 393216 | tf_op jit(solution)/shard_map/all_to_all | solution.py:251
  94.8 0.6 shard_map.106
  (1 shorter events, 0.0 us)
Async XLA Ops:
  0.6 34.7 %copy-start.4 = (s32[192]{0:T(256)S(1)}, s32[192]{0:T(256)}, u32[]{:S(2)}) copy-start(s32[192]{0:T(256)} %constant.2.clone.spots_in) | copy-start | bytes 2308
  0.6 34.7 %copy-start = (bf16[48,128,128]{2,1,0:T(8,128)(2,1)S(1)}, bf16[48,128,128]{2,1,0:T(8,128)(2,1)}, u32[]{:S(2)}) copy-start(bf16[48,128,128]{2,1,0:T(8,128)(2,1)} %tiles_ref.3) | copy-start | bytes 4718596
  0.7 34.7 %copy-start.6 = (s32[48]{0:T(128)S(1)}, s32[48]{0:T(128)}, u32[]{:S(2)}) copy-start(s32[48]{0:T(128)} %cols_in.3) | copy-start | bytes 580
  0.7 34.7 %copy-start.5 = (s32[48]{0:T(128)S(1)}, s32[48]{0:T(128)}, u32[]{:S(2)}) copy-start(s32[48]{0:T(128)} %rows_in.3) | copy-start | bytes 580
  0.7 34.7 %copy-start.1 = (bf16[16,256]{1,0:T(8,128)(2,1)S(1)}, bf16[16,256]{1,0:T(8,128)(2,1)}, u32[]{:S(2)}) copy-start(bf16[16,256]{1,0:T(8,128)(2,1)} %weight_ref.3) | copy-start | bytes 24580
  0.7 34.7 %copy-start.2 = (bf16[256,32]{0,1:T(8,128)(2,1)S(1)}, bf16[256,32]{0,1:T(8,128)(2,1)}, u32[]{:S(2)}) copy-start(bf16[256,32]{0,1:T(8,128)(2,1)} %param.14) | copy-start | bytes 49156
  35.4 30.3 %copy-start.3 = (f32[256]{0:T(256)S(1)}, f32[256]{0:T(256)}, u32[]{:S(2)}) copy-start(f32[256]{0:T(256)} %param.10) | copy-start | bytes 3076
